TPU v7x, 512 devices: a whole 4x8x8 slice. The times are simulated.
512 devices in a mesh: gx: 8 (over y), gy: 8 (over z_lo, core), gz: 8 (over z_hi, x).
Axes of the slice: x: 4, y: 8, z: 8 (z_hi: 2, z_lo: 4; z = z_hi * 4 + z_lo), core: 2. Of those that a mesh axis runs over, the one named last changes fastest.
Arguments:
- acts: bfloat16 [512, 12288], P(('gx', 'gy'), 'gz'), may hold values from -6 to 6
- grad_out: bfloat16 [512, 12288], P(('gx', 'gy'), 'gz'), may hold values from -3 to 3
- w_in: bfloat16 [12288, 24576], P('gz', ('gx', 'gy')), may hold values from -0.0546875 to 0.0546875
- b_in: float32 [24576], P(('gx', 'gy')), may hold values from -3 to 3
- w_out: bfloat16 [24576, 12288], P(('gx', 'gy'), 'gz'), may hold values from -0.0390625 to 0.0390625
Outputs:
- grad_acts: bfloat16 [512, 12288], P(('gx', 'gy'), 'gz')
- grad_w_in: bfloat16 [12288, 24576], P('gz', ('gx', 'gy'))
- grad_b_in: float32 [24576], P(('gx', 'gy'))
- grad_w_out: bfloat16 [24576, 12288], P(('gx', 'gy'), 'gz')
All inputs are finite; a program needn't handle non-finite values.
Results may differ from a plain program's by a relative error of at most 0.007.
Values may be sent and summed in bfloat16 or wider, within the bound.
No kernel may reach another device: no remote copies, remote signals or barrier semaphores. Data moves between devices by JAX's collectives and lax.ppermute only.
A program may use at most 64 MiB of HBM per device.

v0:
```python
import jax
import jax.numpy as jnp
from jax import lax
from jax.sharding import PartitionSpec as P


def activate(preact, back):
    cdf = 0.5 * (1.0 + lax.erf(preact * 0.7071067811865476))
    dens = jnp.exp(-0.5 * preact * preact) * 0.3989422804014327
    activation = (preact * cdf).astype(jnp.bfloat16)
    grad_pre = (back * (cdf + preact * dens)).astype(jnp.bfloat16)
    return (activation, grad_pre)


def contract_rows(left, right):
    return lax.dot_general(
        left, right, (((0,), (0,)), ((), ())), preferred_element_type=jnp.float32
    )


def contract_cols(left, right):
    return lax.dot_general(
        left, right, (((1,), (1,)), ((), ())), preferred_element_type=jnp.float32
    )


def body(acts, grad_out, w_in, b_in, w_out):
    inputs_all, outgrad_all = (
        lax.all_gather(acts, ("gx", "gy"), axis=0, tiled=True),
        lax.all_gather(grad_out, ("gx", "gy"), axis=0, tiled=True),
    )
    pre_part = jnp.dot(inputs_all, w_in, preferred_element_type=jnp.float32)
    back_part = contract_cols(outgrad_all, w_out)
    pre_total, back_total = lax.psum((pre_part, back_part), "gz")
    activation, grad_pre = activate(pre_total + b_in[None, :], back_total)
    grad_w_in = contract_rows(inputs_all, grad_pre).astype(jnp.bfloat16)
    grad_b_in = jnp.sum(grad_pre.astype(jnp.float32), axis=0)
    grad_w_out = contract_rows(activation, outgrad_all).astype(jnp.bfloat16)
    grad_sum = lax.psum_scatter(
        contract_cols(grad_pre, w_in), ("gx", "gy"), scatter_dimension=0, tiled=True
    )
    grad_acts = grad_sum.astype(jnp.bfloat16)
    return (grad_acts, grad_w_in, grad_b_in, grad_w_out)


def solution(mesh):
    return jax.shard_map(
        body,
        mesh=mesh,
        in_specs=(
            P(("gx", "gy"), "gz"),
            P(("gx", "gy"), "gz"),
            P("gz", ("gx", "gy")),
            P(("gx", "gy")),
            P(("gx", "gy"), "gz"),
        ),
        out_specs=(
            P(("gx", "gy"), "gz"),
            P("gz", ("gx", "gy")),
            P(("gx", "gy")),
            P(("gx", "gy"), "gz"),
        ),
        check_vma=False,
    )
```

profile of v0, /device:TPU:1, one launch (start us, length us, event | category | flops | bytes accessed | tf_op | source)
XLA Modules:
  0.0 675.7 jit_solution(12107579492106755065)
XLA Ops:
  7.2 0.0 copy-start
  7.2 0.0 all-gather.3.cloned.1.call-start
  7.2 0.7 all-gather.3.cloned.1.call-update
  7.9 0.0 all-gather.5.cloned.1.call-start
  8.0 0.7 all-gather.5.cloned.1.call-update
  8.7 0.0 all-reduce.3.cloned.1.call-start
  8.7 125.5 %all-gather.3.cloned.1.call-done = bf16[512,1536]{1,0:T(8,128)(2,1)} async-done(((bf16[8,1536]{1,0:T(8,128)(2,1)}), bf16[512,1536]{1,0:T(8,128)(2,1)}) %all-gather.3.cloned.1.call-update) | async-done | bytes 1572880 | tf_op jit(solution)/shard_map/all_gather | solution.py:30
  134.2 3.6 fusion.9
  137.9 114.2 %all-gather.5.cloned.1.call-done = bf16[512,1536]{1,0:T(8,128)(2,1)} async-done(((bf16[8,1536]{1,0:T(8,128)(2,1)}), bf16[512,1536]{1,0:T(8,128)(2,1)}) %all-gather.5.cloned.1.call-update) | async-done | bytes 1572880 | tf_op jit(solution)/shard_map/all_gather | solution.py:29
  252.1 0.0 copy-done
  252.1 3.3 fusion.10
  255.4 0.0 copy-start.2
  255.4 0.0 all-reduce.3.cloned.1.call-update
  255.4 0.0 reduce-scatter.2.cloned.1.call-start
  255.4 124.5 %all-reduce.3.cloned.1.call-done = (f32[512,384]{1,0:T(8,128)}, f32[512,384]{1,0:T(8,128)}) async-done(((f32[512,384]{1,0:T(8,128)}, f32[512,384]{1,0:T(8,128)}), (f32[512,384]{1,0:T(8,128)}, f32[512,384]{1,0:T(8,128)})) %all-reduce.3.cloned.1.call-update) | async-done | bytes 1572880 | tf_op jit(solution)/shard_map/psum | solution.py:34
  380.0 0.0 copy-done.2
  380.0 2.3 convert_reduce_fusion
  382.3 2.7 fusion.11
  385.0 0.0 reduce-scatter.2.cloned.1.call-update
  385.0 2.2 fusion
  387.2 0.0 copy-start.1
  387.2 1.4 copy.9
  388.6 0.0 copy-done.1
  388.6 3.3 convolution_convert_fusion
  391.9 275.9 %reduce-scatter.2.cloned.1.call-done = f32[8,1536]{1,0:T(8,128)} async-done(((f32[512,1536]{1,0:T(8,128)}), f32[8,1536]{1,0:T(8,128)}) %reduce-scatter.2.cloned.1.call-update) | async-done | bytes 49168 | tf_op jit(solution)/shard_map/reduce_scatter | solution.py:39
  667.8 1.4 convert_element_type.22
Async XLA Ops:
  7.2 244.9 %copy-start = (bf16[1536,384]{1,0:T(8,128)(2,1)S(1)}, bf16[1536,384]{1,0:T(8,128)(2,1)}, u32[]{:S(2)}) copy-start(bf16[1536,384]{1,0:T(8,128)(2,1)} %param.7) | copy-start | bytes 3538948
  7.2 127.1 %all-gather.3.cloned.1.call-start = ((), (), s32[]{:S(2)}) async-start(), calls=%async_computation.1 | async-start | bytes 1597440 | tf_op jit(solution)/shard_map/all_gather | solution.py:30
  7.9 244.2 %all-gather.5.cloned.1.call-start = ((), (), s32[]{:S(2)}) async-start(), calls=%async_computation.2 | async-start | bytes 1597440 | tf_op jit(solution)/shard_map/all_gather | solution.py:29
  8.7 371.3 %all-reduce.3.cloned.1.call-start = ((), (), s32[]{:S(2)}) async-start(), calls=%async_computation.4 | async-start | bytes 3145728 | tf_op jit(solution)/shard_map/psum | solution.py:34
  255.4 124.6 %copy-start.2 = (f32[384]{0:T(512)S(1)}, f32[384]{0:T(512)}, u32[]{:S(2)}) copy-start(f32[384]{0:T(512)} %param.8) | copy-start | bytes 4612
  255.4 412.4 %reduce-scatter.2.cloned.1.call-start = ((), (), s32[]{:S(2)}) async-start(), calls=%async_computation.3 | async-start | bytes 3194880 | tf_op jit(solution)/shard_map/reduce_scatter | solution.py:39
  387.2 1.4 copy-start.1
Sparse Core Ops, SparseCore 0:
  10.2 124.0 all-gather.2
  136.4 115.6 all-gather.4
  255.7 124.2 all-reduce.2
  385.1 282.6 reduce-scatter.1
where the time goes:
time: 680 us; the launch traced here: 676 us
  waiting for transfers between devices  642 us (94%)
  matrix products  15 us (2%)
  between operations  13.8 us (2%)
    reduce_scatter x1, waiting for transfers between devices, body(): lax.psum_scatter(contract_cols(grad_pre, w_in), ('gx', 'gy'), scatter_dim...  276 us
    all_gather x1, waiting for transfers between devices, body(): lax.all_gather(grad_out, ('gx', 'gy'), axis=0, tiled=True)  126 us
    psum x1, waiting for transfers between devices, body(): pre_total, back_total = lax.psum((pre_part, back_part), 'gz')  125 us
    all_gather x1, waiting for transfers between devices, body(): lax.all_gather(acts, ('gx', 'gy'), axis=0, tiled=True)  114 us
  transfers between devices with their start and end apart: 4, of which 4 were waited for; matrix products, arithmetic and copies ran while one was open for 2% of the time, Pallas kernels for 0%

commit v1 on v0

v1 whole, which is shorter than its diff:
```python
import jax
import jax.numpy as jnp
from jax import lax
from jax.sharding import Mesh, PartitionSpec as P

BF16 = jnp.bfloat16
F32 = jnp.float32
PLANE = ("y", "zl")
MODEL = ("zh", "x")


def activate(preact, back):
    cdf = 0.5 * (1.0 + lax.erf(preact * 0.7071067811865476))
    dens = jnp.exp(-0.5 * preact * preact) * 0.3989422804014327
    activation = (preact * cdf).astype(BF16)
    grad_pre = (back * (cdf + preact * dens)).astype(BF16)
    return activation, grad_pre


def contract_rows(left, right):
    return lax.dot_general(
        left, right, (((0,), (0,)), ((), ())), preferred_element_type=F32
    )


def contract_cols(left, right):
    return lax.dot_general(
        left, right, (((1,), (1,)), ((), ())), preferred_element_type=F32
    )


def swap_cores(value):
    return lax.ppermute(value, "co", [(0, 1), (1, 0)])


def gather_blocks(value, axes):
    count = lax.axis_size(axes)
    copies = jnp.broadcast_to(value[None], (count, *value.shape))
    return lax.all_to_all(copies, axes, 0, 0, tiled=True)


def gather_tokens(value):
    own = gather_blocks(value, PLANE).reshape(-1, value.shape[1])
    return jnp.concatenate([own, swap_cores(own)], axis=0)


def sum_blocks(value, axes):
    count = lax.axis_size(axes)
    blocks = value.astype(BF16).reshape(count, value.shape[0] // count, value.shape[1])
    blocks = lax.all_to_all(blocks, axes, 0, 0, tiled=True)
    return jnp.sum(blocks.astype(F32), axis=0)


def body(acts, grad_out, w_in, b_in, w_out):
    inputs_all = gather_tokens(acts)
    outgrad_all = gather_tokens(grad_out)
    preact = sum_blocks(jnp.dot(inputs_all, w_in, preferred_element_type=F32), MODEL)
    back = sum_blocks(contract_cols(outgrad_all, w_out), MODEL)
    activation, grad_pre = activate(preact + b_in[None, :], back)
    width = b_in.shape[0]
    grad_pre = gather_blocks(grad_pre, MODEL).reshape(-1, width)
    activation = gather_blocks(activation, MODEL).reshape(-1, width)
    grad_w_in = contract_rows(inputs_all, grad_pre).astype(BF16)
    grad_b_in = jnp.sum(grad_pre.astype(F32), axis=0)
    grad_w_out = contract_rows(activation, outgrad_all).astype(BF16)
    partial = contract_cols(grad_pre, w_in)
    half = partial.shape[0] // 2
    partial = partial[:half] + swap_cores(partial[half:].astype(BF16)).astype(F32)
    grad_acts = sum_blocks(partial, PLANE).astype(BF16)
    return (grad_acts, grad_w_in, grad_b_in, grad_w_out)


def solution(mesh):
    fine = Mesh(mesh.devices.reshape(8, 4, 2, 2, 4), ("y", "zl", "co", "zh", "x"))
    tokens = ("y", "zl", "co")
    return jax.shard_map(
        body,
        mesh=fine,
        in_specs=(
            P(tokens, MODEL),
            P(tokens, MODEL),
            P(MODEL, tokens),
            P(tokens),
            P(tokens, MODEL),
        ),
        out_specs=(
            P(tokens, MODEL),
            P(MODEL, tokens),
            P(tokens),
            P(tokens, MODEL),
        ),
        check_vma=False,
    )
```

time: 680 us -> 187 us (0.28)
  waiting for transfers between devices: 642 us -> 62.5 us
  starting transfers between devices: 0.16 us -> 51.9 us
  blocking collectives: 0 us -> 48.5 us
  between operations: 13.8 us -> 0.8 us
    reduce_scatter x1 -> x0, waiting for transfers between devices: 276 us -> none  [body(): lax.psum_scatter(contract_cols(grad_pre, w_in), ('gx', 'gy'), scatter_dim...]
    all_gather x2 -> x0, waiting for transfers between devices: 240 us -> none  [the longest x1 126 us: body(): lax.all_gather(grad_out, ('gx', 'gy'), axis=0, tiled=True)]
    psum x1 -> x0, waiting for transfers between devices: 125 us -> none  [body(): pre_total, back_total = lax.psum((pre_part, back_part), 'gz')]
    all_to_all x0 -> x5, waiting for transfers between devices: none -> 62.5 us  [the longest x3 34.8 us: sum_blocks(): blocks = lax.all_to_all(blocks, axes, 0, 0, tiled=True)]
    all_to_all x0 -> x2, blocking collectives: none -> 48.5 us  [gather_blocks(): return lax.all_to_all(copies, axes, 0, 0, tiled=True)]
    all_to_all x0 -> x5, starting transfers between devices: none -> 33.9 us  [the longest x3 24.1 us: sum_blocks(): blocks = lax.all_to_all(blocks, axes, 0, 0, tiled=True)]
    ppermute x0 -> x3, starting transfers between devices: none -> 18 us  [swap_cores(): return lax.ppermute(value, 'co', [(0, 1), (1, 0)])]
  transfers between devices with their start and end apart: 4 -> 8, of which waited for: 4 -> 5; matrix products, arithmetic and copies ran while one was open for 2% -> 8% of each run, Pallas kernels for 0% -> 0%
where the time goes in v1:
time: 187 us; the launch traced here: 185 us
  waiting for transfers between devices  62.5 us (33%)
  starting transfers between devices  51.9 us (28%)
  blocking collectives  48.5 us (26%)
  matrix products  12.4 us (7%)
  local copies, waits for them, and re-layouts  4.38 us (2%)
  other arithmetic  4.33 us (2%)
    all_to_all x2, blocking collectives, gather_blocks(): return lax.all_to_all(copies, axes, 0, 0, tiled=True)  48.5 us
    all_to_all x3, waiting for transfers between devices, sum_blocks(): blocks = lax.all_to_all(blocks, axes, 0, 0, tiled=True)  34.8 us
    all_to_all x2, waiting for transfers between devices, gather_blocks(): return lax.all_to_all(copies, axes, 0, 0, tiled=True)  27.7 us
    all_to_all x3, starting transfers between devices, sum_blocks(): blocks = lax.all_to_all(blocks, axes, 0, 0, tiled=True)  24.1 us
    ppermute x3, starting transfers between devices, swap_cores(): return lax.ppermute(value, 'co', [(0, 1), (1, 0)])  18 us
    all_to_all x2, starting transfers between devices, gather_blocks(): return lax.all_to_all(copies, axes, 0, 0, tiled=True)  9.77 us
    dot_general x2, matrix products, contract_rows(): lax.dot_general(left, right, (((0,), (0,)), ((), ())), preferred_element_...  5.28 us
    dot_general x2, matrix products, contract_cols(): lax.dot_general(left, right, (((1,), (1,)), ((), ())), preferred_element_...  4.29 us
  transfers between devices with their start and end apart: 8, of which 5 were waited for; matrix products, arithmetic and copies ran while one was open for 8% of the time, Pallas kernels for 0%

profile of v1, /device:TPU:1, one launch (start us, length us, event | category | flops | bytes accessed | tf_op | source)
XLA Modules:
  0.0 184.9 jit_solution(4476315165620175559)
XLA Ops:
  0.6 0.0 copy-start
  0.7 0.9 broadcast_in_dim.8
  1.5 34.8 %all_to_all.35 = bf16[32,8,1536]{2,1,0:T(8,128)(2,1)S(1)} all-to-all(bf16[32,8,1536]{2,1,0:T(8,128)(2,1)S(1)} %broadcast_in_dim.8), channel_id=1, replica_groups=mesh['y'=8,'zl'=4,'co'=2,'zh'=2,'x'=4] {'y','zl'}, dimensions={0} | all-to-all | bytes 1572864 | tf_op jit(solution)/shard_map/all_to_all | solution.py:39
  36.4 0.9 broadcast_in_dim.9
  37.3 6.3 %all-to-all-start.2 = ((bf16[32,8,1536]{2,1,0:T(8,128)(2,1)}), bf16[32,8,1536]{2,1,0:T(8,128)(2,1)S(1)}, u32[]{:S(2)}, u32[]{:S(2)}) async-start(bf16[32,8,1536]{2,1,0:T(8,128)(2,1)} %broadcast_in_dim.9), calls=%async_computation.2 | async-start | bytes 1572864 | tf_op jit(solution)/shard_map/all_to_all | solution.py:39
  43.6 2.7 %collective-permute-start = (bf16[256,1536]{1,0:T(8,128)(2,1)S(1)}, bf16[256,1536]{1,0:T(8,128)(2,1)S(1)}, u32[]{:S(2)}, u32[]{:S(2)}) collective-permute-start(bf16[256,1536]{1,0:T(8,128)(2,1)S(1)} %bitcast.16), channel_id=1, source_target_pairs={{0,8},{8,0},{1,9},{9,1},{2,10},{10,2},{3,11},{11,3},{4,12},{12,4},... | collective-permute-start | bytes 2359304 | tf_op jit(solution)/shard_map/ppermute | solution.py:33
  46.4 18.8 %all-to-all-done.2 = bf16[32,8,1536]{2,1,0:T(8,128)(2,1)S(1)} async-done(((bf16[32,8,1536]{2,1,0:T(8,128)(2,1)}), bf16[32,8,1536]{2,1,0:T(8,128)(2,1)S(1)}, u32[]{:S(2)}, u32[]{:S(2)}) %all-to-all-start.2) | async-done | bytes 786464 | tf_op jit(solution)/shard_map/all_to_all | solution.py:39
  65.2 5.0 %collective-permute-start.1 = (bf16[256,1536]{1,0:T(8,128)(2,1)S(1)}, bf16[256,1536]{1,0:T(8,128)(2,1)}, u32[]{:S(2)}, u32[]{:S(2)}) collective-permute-start(bf16[256,1536]{1,0:T(8,128)(2,1)S(1)} %bitcast.19), channel_id=1, source_target_pairs={{0,8},{8,0},{1,9},{9,1},{2,10},{10,2},{3,11},{11,3},{4,12},{12,4},... | collective-permute-start | bytes 2359304 | tf_op jit(solution)/shard_map/ppermute | solution.py:33
  70.1 3.3 %convolution_convert_fusion.3 = bf16[512,384]{1,0:T(8,128)(2,1)} fusion(bf16[384,1536]{1,0:T(8,128)(2,1)} %param.9, bf16[256,1536]{1,0:T(8,128)(2,1)S(1)} %collective-permute-done, bf16[256,1536]{1,0:T(8,128)(2,1)S(1)} %bitcast.17), kind=kOutput, calls=%fused_computation.8 | convolution fusion | flops 607322112 | bytes 3145728 | tf_op jit(solution)/shard_map/dot_general | solution.py:27
  73.4 9.8 %all-to-all-start.1 = ((bf16[8,64,384]{2,1,0:T(8,128)(2,1)}), bf16[8,64,384]{2,1,0:T(8,128)(2,1)S(1)}, u32[]{:S(2)}, u32[]{:S(2)}) async-start(bf16[8,64,384]{2,1,0:T(8,128)(2,1)} %bitcast.1), calls=%async_computation.1 | async-start | bytes 786432 | tf_op jit(solution)/shard_map/all_to_all | solution.py:50
  83.2 2.9 %convolution_convert_fusion.2 = bf16[512,384]{1,0:T(8,128)(2,1)} fusion(bf16[1536,384]{1,0:T(8,128)(2,1)S(1)} %copy-done, bf16[256,1536]{1,0:T(8,128)(2,1)} %collective-permute-done.1, bf16[256,1536]{1,0:T(8,128)(2,1)S(1)} %bitcast.20), kind=kOutput, calls=%fused_computation.7 | convolution fusion | flops 607322112 | bytes 3145728 | tf_op jit(solution)/shard_map/dot_general | solution.py:57
  86.1 8.7 %all-to-all-done.1 = bf16[8,64,384]{2,1,0:T(8,128)(2,1)S(1)} async-done(((bf16[8,64,384]{2,1,0:T(8,128)(2,1)}), bf16[8,64,384]{2,1,0:T(8,128)(2,1)S(1)}, u32[]{:S(2)}, u32[]{:S(2)}) %all-to-all-start.1) | async-done | bytes 393248 | tf_op jit(solution)/shard_map/all_to_all | solution.py:50
  94.8 3.9 %all-to-all-start.3 = ((bf16[8,64,384]{2,1,0:T(8,128)(2,1)}), bf16[8,64,384]{2,1,0:T(8,128)(2,1)S(1)}, u32[]{:S(2)}, u32[]{:S(2)}) async-start(bf16[8,64,384]{2,1,0:T(8,128)(2,1)} %bitcast.3), calls=%async_computation.3 | async-start | bytes 786432 | tf_op jit(solution)/shard_map/all_to_all | solution.py:50
  98.7 0.1 convert_reduce_fusion.2
  98.7 10.5 %all-to-all-done.3 = bf16[8,64,384]{2,1,0:T(8,128)(2,1)S(1)} async-done(((bf16[8,64,384]{2,1,0:T(8,128)(2,1)}), bf16[8,64,384]{2,1,0:T(8,128)(2,1)S(1)}, u32[]{:S(2)}, u32[]{:S(2)}) %all-to-all-start.3) | async-done | bytes 393248 | tf_op jit(solution)/shard_map/all_to_all | solution.py:50
  109.2 0.1 convert_reduce_fusion.1
  109.2 0.1 multiply_convert_fusion
  109.3 13.7 %all_to_all.36 = bf16[8,64,384]{2,1,0:T(8,128)(2,1)S(1)} all-to-all(bf16[8,64,384]{2,1,0:T(8,128)(2,1)S(1)} %broadcast_in_dim.10), channel_id=1, replica_groups=mesh['y'=8,'zl'=4,'co'=2,'zh'=2,'x'=4] {'zh','x'}, dimensions={0} | all-to-all | bytes 786432 | tf_op jit(solution)/shard_map/all_to_all | solution.py:39
  123.0 1.0 fusion.12
  124.0 1.6 copy-done.1
  125.7 0.1 slice.17
  125.7 10.3 %collective-permute-start.2 = (bf16[256,1536]{1,0:T(8,128)(2,1)S(1)}, bf16[256,1536]{1,0:T(8,128)(2,1)}, u32[]{:S(2)}, u32[]{:S(2)}) collective-permute-start(bf16[256,1536]{1,0:T(8,128)(2,1)S(1)} %slice.17), channel_id=1, source_target_pairs={{0,8},{8,0},{1,9},{9,1},{2,10},{10,2},{3,11},{11,3},{4,12},{12,4},... | collective-permute-start | bytes 2359304 | tf_op jit(solution)/shard_map/ppermute | solution.py:33
  136.1 0.8 broadcast_in_dim.11
  136.9 3.5 %all-to-all-start.6 = ((bf16[8,64,384]{2,1,0:T(8,128)(2,1)}), bf16[8,64,384]{2,1,0:T(8,128)(2,1)S(1)}, u32[]{:S(2)}, u32[]{:S(2)}) async-start(bf16[8,64,384]{2,1,0:T(8,128)(2,1)} %broadcast_in_dim.11), calls=%async_computation.6 | async-start | bytes 786432 | tf_op jit(solution)/shard_map/all_to_all | solution.py:39
  140.4 2.8 %fusion.1 = bf16[32,8,1536]{2,1,0:T(8,128)(2,1)} fusion(bf16[256,1536]{1,0:T(8,128)(2,1)} %collective-permute-done.2, f32[512,1536]{1,0:T(8,128)} %copy-done.1), kind=kLoop, calls=%fused_computation.9 | loop fusion | flops 1179648 | bytes 3145728 | tf_op jit(solution)/shard_map/reshape | solution.py:49
  143.1 9.0 %all-to-all-done.6 = bf16[8,64,384]{2,1,0:T(8,128)(2,1)S(1)} async-done(((bf16[8,64,384]{2,1,0:T(8,128)(2,1)}), bf16[8,64,384]{2,1,0:T(8,128)(2,1)S(1)}, u32[]{:S(2)}, u32[]{:S(2)}) %all-to-all-start.6) | async-done | bytes 393248 | tf_op jit(solution)/shard_map/all_to_all | solution.py:39
  152.1 10.5 %all-to-all-start.5 = ((bf16[32,8,1536]{2,1,0:T(8,128)(2,1)}), bf16[32,8,1536]{2,1,0:T(8,128)(2,1)S(1)}, u32[]{:S(2)}, u32[]{:S(2)}) async-start(bf16[32,8,1536]{2,1,0:T(8,128)(2,1)} %fusion.1), calls=%async_computation.5 | async-start | bytes 1572864 | tf_op jit(solution)/shard_map/all_to_all | solution.py:50
  162.6 0.7 convert_reduce_fusion
  163.2 3.5 %convolution_convert_fusion.1 = bf16[1536,384]{1,0:T(8,128)(2,1)} fusion(bf16[512,384]{1,0:T(8,128)(2,1)S(1)} %bitcast.15, bf16[256,1536]{1,0:T(8,128)(2,1)} %collective-permute-done.1, bf16[256,1536]{1,0:T(8,128)(2,1)} %bitcast.21), kind=kOutput, calls=%fused_computation.1 | convolution fusion | flops 607715328 | bytes 3145728 | tf_op jit(solution)/shard_map/dot_general | solution.py:21
  166.7 1.8 convolution_convert_fusion
  168.5 15.6 %all-to-all-done.5 = bf16[32,8,1536]{2,1,0:T(8,128)(2,1)S(1)} async-done(((bf16[32,8,1536]{2,1,0:T(8,128)(2,1)}), bf16[32,8,1536]{2,1,0:T(8,128)(2,1)S(1)}, u32[]{:S(2)}, u32[]{:S(2)}) %all-to-all-start.5) | async-done | bytes 786464 | tf_op jit(solution)/shard_map/all_to_all | solution.py:50
  184.2 0.7 reduce_sum.41
  (16 shorter events, 0.1 us)
Async XLA Ops:
  0.6 82.6 %copy-start = (bf16[1536,384]{1,0:T(8,128)(2,1)S(1)}, bf16[1536,384]{1,0:T(8,128)(2,1)}, u32[]{:S(2)}) copy-start(bf16[1536,384]{1,0:T(8,128)(2,1)} %param.7) | copy-start | bytes 3538948
  0.6 35.7 %copy-start.3 = (bf16[8,1536]{1,0:T(8,128)(2,1)S(1)}, bf16[8,1536]{1,0:T(8,128)(2,1)}, u32[]{:S(2)}) copy-start(bf16[8,1536]{1,0:T(8,128)(2,1)} %param.5) | copy-start | bytes 73732
  37.3 27.8 %all-to-all-start.2 = ((bf16[32,8,1536]{2,1,0:T(8,128)(2,1)}), bf16[32,8,1536]{2,1,0:T(8,128)(2,1)S(1)}, u32[]{:S(2)}, u32[]{:S(2)}) async-start(bf16[32,8,1536]{2,1,0:T(8,128)(2,1)} %broadcast_in_dim.9), calls=%async_computation.2 | async-start | bytes 1572864 | tf_op jit(solution)/shard_map/all_to_all | solution.py:39
  43.6 26.5 %collective-permute-start = (bf16[256,1536]{1,0:T(8,128)(2,1)S(1)}, bf16[256,1536]{1,0:T(8,128)(2,1)S(1)}, u32[]{:S(2)}, u32[]{:S(2)}) collective-permute-start(bf16[256,1536]{1,0:T(8,128)(2,1)S(1)} %bitcast.16), channel_id=1, source_target_pairs={{0,8},{8,0},{1,9},{9,1},{2,10},{10,2},{3,11},{11,3},{4,12},{12,4},... | collective-permute-start | bytes 2359304 | tf_op jit(solution)/shard_map/ppermute | solution.py:33
  65.2 18.1 %copy-start.2 = (bf16[32,8,1536]{2,1,0:T(8,128)(2,1)}, bf16[32,8,1536]{2,1,0:T(8,128)(2,1)S(1)}, u32[]{:S(2)}) copy-start(bf16[32,8,1536]{2,1,0:T(8,128)(2,1)S(1)} %all-to-all-done.2) | copy-start | bytes 2359300
  65.2 18.1 %collective-permute-start.1 = (bf16[256,1536]{1,0:T(8,128)(2,1)S(1)}, bf16[256,1536]{1,0:T(8,128)(2,1)}, u32[]{:S(2)}, u32[]{:S(2)}) collective-permute-start(bf16[256,1536]{1,0:T(8,128)(2,1)S(1)} %bitcast.19), channel_id=1, source_target_pairs={{0,8},{8,0},{1,9},{9,1},{2,10},{10,2},{3,11},{11,3},{4,12},{12,4},... | collective-permute-start | bytes 2359304 | tf_op jit(solution)/shard_map/ppermute | solution.py:33
  70.1 3.3 %copy-start.5 = (bf16[256,1536]{1,0:T(8,128)(2,1)}, bf16[256,1536]{1,0:T(8,128)(2,1)S(1)}, u32[]{:S(2)}) copy-start(bf16[256,1536]{1,0:T(8,128)(2,1)S(1)} %collective-permute-done) | copy-start | bytes 2359300
  73.4 21.4 %all-to-all-start.1 = ((bf16[8,64,384]{2,1,0:T(8,128)(2,1)}), bf16[8,64,384]{2,1,0:T(8,128)(2,1)S(1)}, u32[]{:S(2)}, u32[]{:S(2)}) async-start(bf16[8,64,384]{2,1,0:T(8,128)(2,1)} %bitcast.1), calls=%async_computation.1 | async-start | bytes 786432 | tf_op jit(solution)/shard_map/all_to_all | solution.py:50
  86.1 23.1 %copy-start.4 = (f32[384]{0:T(512)S(1)}, f32[384]{0:T(512)}, u32[]{:S(2)}) copy-start(f32[384]{0:T(512)} %param.8) | copy-start | bytes 4612
  94.8 14.4 %all-to-all-start.3 = ((bf16[8,64,384]{2,1,0:T(8,128)(2,1)}), bf16[8,64,384]{2,1,0:T(8,128)(2,1)S(1)}, u32[]{:S(2)}, u32[]{:S(2)}) async-start(bf16[8,64,384]{2,1,0:T(8,128)(2,1)} %bitcast.3), calls=%async_computation.3 | async-start | bytes 786432 | tf_op jit(solution)/shard_map/all_to_all | solution.py:50
  124.0 1.6 copy-start.1
  125.7 14.6 %collective-permute-start.2 = (bf16[256,1536]{1,0:T(8,128)(2,1)S(1)}, bf16[256,1536]{1,0:T(8,128)(2,1)}, u32[]{:S(2)}, u32[]{:S(2)}) collective-permute-start(bf16[256,1536]{1,0:T(8,128)(2,1)S(1)} %slice.17), channel_id=1, source_target_pairs={{0,8},{8,0},{1,9},{9,1},{2,10},{10,2},{3,11},{11,3},{4,12},{12,4},... | collective-permute-start | bytes 2359304 | tf_op jit(solution)/shard_map/ppermute | solution.py:33
  136.9 15.2 %all-to-all-start.6 = ((bf16[8,64,384]{2,1,0:T(8,128)(2,1)}), bf16[8,64,384]{2,1,0:T(8,128)(2,1)S(1)}, u32[]{:S(2)}, u32[]{:S(2)}) async-start(bf16[8,64,384]{2,1,0:T(8,128)(2,1)} %broadcast_in_dim.11), calls=%async_computation.6 | async-start | bytes 786432 | tf_op jit(solution)/shard_map/all_to_all | solution.py:39
  152.1 32.1 %all-to-all-start.5 = ((bf16[32,8,1536]{2,1,0:T(8,128)(2,1)}), bf16[32,8,1536]{2,1,0:T(8,128)(2,1)S(1)}, u32[]{:S(2)}, u32[]{:S(2)}) async-start(bf16[32,8,1536]{2,1,0:T(8,128)(2,1)} %fusion.1), calls=%async_computation.5 | async-start | bytes 1572864 | tf_op jit(solution)/shard_map/all_to_all | solution.py:50
  163.2 3.5 %copy-start.6 = (bf16[256,1536]{1,0:T(8,128)(2,1)S(1)}, bf16[256,1536]{1,0:T(8,128)(2,1)}, u32[]{:S(2)}) copy-start(bf16[256,1536]{1,0:T(8,128)(2,1)} %copy-done.5) | copy-start | bytes 2359300

commit v2 on v1

--- a/solution.py
+++ b/solution.py
@@ -36,37 +36,42 @@
 def gather_blocks(value, axes):
     count = lax.axis_size(axes)
     copies = jnp.broadcast_to(value[None], (count, *value.shape))
-    return lax.all_to_all(copies, axes, 0, 0, tiled=True)
-
-
-def gather_tokens(value):
-    own = gather_blocks(value, PLANE).reshape(-1, value.shape[1])
-    return jnp.concatenate([own, swap_cores(own)], axis=0)
+    return lax.all_to_all(copies, axes, 0, 0, tiled=True).reshape(-1, value.shape[1])
 
 
 def sum_blocks(value, axes):
     count = lax.axis_size(axes)
-    blocks = value.astype(BF16).reshape(count, value.shape[0] // count, value.shape[1])
+    blocks = value.reshape(count, value.shape[0] // count, value.shape[1])
     blocks = lax.all_to_all(blocks, axes, 0, 0, tiled=True)
     return jnp.sum(blocks.astype(F32), axis=0)
 
 
+def sum_model(value):
+    value = sum_blocks(value, "x").astype(BF16)
+    other = lax.ppermute(value, "zh", [(0, 1), (1, 0)])
+    return value.astype(F32) + other.astype(F32)
+
+
 def body(acts, grad_out, w_in, b_in, w_out):
-    inputs_all = gather_tokens(acts)
-    outgrad_all = gather_tokens(grad_out)
-    preact = sum_blocks(jnp.dot(inputs_all, w_in, preferred_element_type=F32), MODEL)
-    back = sum_blocks(contract_cols(outgrad_all, w_out), MODEL)
-    activation, grad_pre = activate(preact + b_in[None, :], back)
-    width = b_in.shape[0]
-    grad_pre = gather_blocks(grad_pre, MODEL).reshape(-1, width)
-    activation = gather_blocks(activation, MODEL).reshape(-1, width)
+    width, hidden = w_in.shape
+    own = gather_blocks(jnp.concatenate([acts, grad_out], axis=1), PLANE)
+    both = jnp.concatenate([own, swap_cores(own)], axis=0)
+    inputs_all, outgrad_all = both[:, :width], both[:, width:]
+    preact = jnp.dot(inputs_all, w_in, preferred_element_type=F32).astype(BF16)
+    back = contract_cols(outgrad_all, w_out).astype(BF16)
+    sums = sum_model(jnp.concatenate([preact, back], axis=1))
+    activation, grad_pre = activate(
+        sums[:, :hidden] + b_in[None, :], sums[:, hidden:]
+    )
+    results = gather_blocks(jnp.concatenate([activation, grad_pre], axis=1), "x")
+    activation, grad_pre = results[:, :hidden], results[:, hidden:]
+    half = grad_pre.shape[0] // 2
+    other = swap_cores(contract_cols(grad_pre[half:], w_in).astype(BF16))
+    partial = contract_cols(grad_pre[:half], w_in) + other.astype(F32)
+    grad_acts = sum_blocks(partial.astype(BF16), PLANE).astype(BF16)
     grad_w_in = contract_rows(inputs_all, grad_pre).astype(BF16)
     grad_b_in = jnp.sum(grad_pre.astype(F32), axis=0)
     grad_w_out = contract_rows(activation, outgrad_all).astype(BF16)
-    partial = contract_cols(grad_pre, w_in)
-    half = partial.shape[0] // 2
-    partial = partial[:half] + swap_cores(partial[half:].astype(BF16)).astype(F32)
-    grad_acts = sum_blocks(partial, PLANE).astype(BF16)
     return (grad_acts, grad_w_in, grad_b_in, grad_w_out)
 
 

time: 187 us -> 145 us (0.78)
  waiting for transfers between devices: 62.5 us -> 24 us
  blocking collectives: 48.5 us -> 78.1 us
  starting transfers between devices: 51.9 us -> 28.4 us
  local copies, waits for them, and re-layouts: 4.38 us -> 0.71 us
  matrix products: 12.4 us -> 9.07 us
    all_to_all x2 -> x3, blocking collectives: 48.5 us -> 78.1 us  [the longest x2 62.8 us: gather_blocks(): lax.all_to_all(copies, axes, 0, 0, tiled=True).reshape(-1, value.shape[1])]
    all_to_all x2 -> x0, waiting for transfers between devices: 27.7 us -> none  [gather_blocks(): return lax.all_to_all(copies, axes, 0, 0, tiled=True)]
    all_to_all x3 -> x1, waiting for transfers between devices: 34.8 us -> 15.7 us  [sum_blocks(): blocks = lax.all_to_all(blocks, axes, 0, 0, tiled=True)]
    all_to_all x3 -> x1, starting transfers between devices: 24.1 us -> 7.52 us  [sum_blocks(): blocks = lax.all_to_all(blocks, axes, 0, 0, tiled=True)]
    all_to_all x2 -> x0, starting transfers between devices: 9.77 us -> none  [gather_blocks(): return lax.all_to_all(copies, axes, 0, 0, tiled=True)]
    ppermute x0 -> x1, starting transfers between devices: none -> 7.95 us  [sum_model(): other = lax.ppermute(value, 'zh', [(0, 1), (1, 0)])]
    ppermute x3 -> x2, starting transfers between devices: 18 us -> 13 us  [swap_cores(): return lax.ppermute(value, 'co', [(0, 1), (1, 0)])]
    ppermute x3 -> x2, waiting for transfers between devices: 0.01 us -> 4.9 us  [swap_cores(): return lax.ppermute(value, 'co', [(0, 1), (1, 0)])]
  transfers between devices with their start and end apart: 8 -> 4, of which waited for: 5 -> 4; matrix products, arithmetic and copies ran while one was open for 8% -> 4% of each run, Pallas kernels for 0% -> 0%
where the time goes in v2:
time: 145 us; the launch traced here: 144 us
  blocking collectives  78.1 us (54%)
  starting transfers between devices  28.4 us (20%)
  waiting for transfers between devices  24 us (17%)
  matrix products  9.07 us (6%)
  other arithmetic  2.89 us (2%)
    all_to_all x2, blocking collectives, gather_blocks(): lax.all_to_all(copies, axes, 0, 0, tiled=True).reshape(-1, value.shape[1])  62.8 us
    all_to_all x1, waiting for transfers between devices, sum_blocks(): blocks = lax.all_to_all(blocks, axes, 0, 0, tiled=True)  15.7 us
    all_to_all x1, blocking collectives, sum_blocks(): blocks = lax.all_to_all(blocks, axes, 0, 0, tiled=True)  15.2 us
    ppermute x2, starting transfers between devices, swap_cores(): return lax.ppermute(value, 'co', [(0, 1), (1, 0)])  13 us
    ppermute x1, starting transfers between devices, sum_model(): other = lax.ppermute(value, 'zh', [(0, 1), (1, 0)])  7.95 us
    all_to_all x1, starting transfers between devices, sum_blocks(): blocks = lax.all_to_all(blocks, axes, 0, 0, tiled=True)  7.52 us
    dot_general x2, matrix products, contract_rows(): lax.dot_general(left, right, (((0,), (0,)), ((), ())), preferred_element_...  5.36 us
    ppermute x2, waiting for transfers between devices, swap_cores(): return lax.ppermute(value, 'co', [(0, 1), (1, 0)])  4.9 us
  transfers between devices with their start and end apart: 4, of which 4 were waited for; matrix products, arithmetic and copies ran while one was open for 4% of the time, Pallas kernels for 0%

profile of v2, /device:TPU:1, one launch (start us, length us, event | category | flops | bytes accessed | tf_op | source)
XLA Modules:
  0.0 143.9 jit_solution(8682982956039110595)
XLA Ops:
  0.6 0.0 copy-start
  0.6 0.9 pad_maximum_fusion.4
  1.5 0.2 broadcast_in_dim.4
  1.7 52.1 %all_to_all.20 = bf16[32,8,3072]{2,1,0:T(8,128)(2,1)S(1)} all-to-all(bf16[32,8,3072]{2,1,0:T(8,128)(2,1)S(1)} %broadcast_in_dim.4), channel_id=1, replica_groups=mesh['y'=8,'zl'=4,'co'=2,'zh'=2,'x'=4] {'y','zl'}, dimensions={0} | all-to-all | bytes 3145728 | tf_op jit(solution)/shard_map/all_to_all | solution.py:39
  53.8 5.2 %collective-permute-start = (bf16[256,3072]{1,0:T(8,128)(2,1)S(1)}, bf16[256,3072]{1,0:T(8,128)(2,1)S(1)}, u32[]{:S(2)}, u32[]{:S(2)}) collective-permute-start(bf16[256,3072]{1,0:T(8,128)(2,1)S(1)} %bitcast.18), channel_id=1, source_target_pairs={{0,8},{8,0},{1,9},{9,1},{2,10},{10,2},{3,11},{11,3},{4,12},{12,4},... | collective-permute-start | bytes 4718600 | tf_op jit(solution)/shard_map/ppermute | solution.py:33
  59.0 3.0 %collective-permute-done = bf16[256,3072]{1,0:T(8,128)(2,1)S(1)} collective-permute-done((bf16[256,3072]{1,0:T(8,128)(2,1)S(1)}, bf16[256,3072]{1,0:T(8,128)(2,1)S(1)}, u32[]{:S(2)}, u32[]{:S(2)}) %collective-permute-start) | collective-permute-done | bytes 1572896 | tf_op jit(solution)/shard_map/ppermute | solution.py:33
  62.0 0.0 copy-done
  62.0 0.8 convolution_convert_fusion.4
  62.8 0.3 copy-done.4
  63.2 0.0 copy-done.6
  63.2 0.8 convolution_convert_fusion.3
  64.0 0.1 copy_bitcast_fusion
  64.1 0.0 copy-start.3
  64.1 15.2 %all_to_all.21 = bf16[4,128,768]{1,2,0:T(8,128)(2,1)S(1)} all-to-all(bf16[4,128,768]{1,2,0:T(8,128)(2,1)S(1)} %copy_bitcast_fusion), channel_id=1, replica_groups=mesh['y'=8,'zl'=4,'co'=2,'zh'=2,'x'=4] {'x'}, dimensions={0} | all-to-all | bytes 1572864 | tf_op jit(solution)/shard_map/all_to_all | solution.py:45
  79.4 0.2 reduce_sum.33
  79.5 8.0 %collective-permute-start.1 = (bf16[128,768]{0,1:T(8,128)(2,1)S(1)}, bf16[128,768]{0,1:T(8,128)(2,1)S(1)}, u32[]{:S(2)}, u32[]{:S(2)}) collective-permute-start(bf16[128,768]{0,1:T(8,128)(2,1)S(1)} %reduce_sum.33), channel_id=1, source_target_pairs={{0,4},{4,0},{1,5},{5,1},{2,6},{6,2},{3,7},{7,3},{8,12},{12,8},{9,1... | collective-permute-start | bytes 589832 | tf_op jit(solution)/shard_map/ppermute | solution.py:51
  87.5 3.4 %collective-permute-done.1 = bf16[128,768]{0,1:T(8,128)(2,1)S(1)} collective-permute-done((bf16[128,768]{0,1:T(8,128)(2,1)S(1)}, bf16[128,768]{0,1:T(8,128)(2,1)S(1)}, u32[]{:S(2)}, u32[]{:S(2)}) %collective-permute-start.1) | collective-permute-done | bytes 196640 | tf_op jit(solution)/shard_map/ppermute | solution.py:51
  90.9 0.1 multiply_convert_fusion
  91.1 0.1 fusion.9
  91.2 0.1 copy.14
  91.4 0.1 broadcast_in_dim.5
  91.5 10.7 %all_to_all.22 = bf16[4,128,768]{2,1,0:T(8,128)(2,1)S(1)} all-to-all(bf16[4,128,768]{2,1,0:T(8,128)(2,1)S(1)} %broadcast_in_dim.5), channel_id=1, replica_groups=mesh['y'=8,'zl'=4,'co'=2,'zh'=2,'x'=4] {'x'}, dimensions={0} | all-to-all | bytes 1572864 | tf_op jit(solution)/shard_map/all_to_all | solution.py:39
  102.2 0.6 convolution_convert_fusion.2
  102.8 7.8 %collective-permute-start.2 = (bf16[256,1536]{1,0:T(8,128)(2,1)S(1)}, bf16[256,1536]{1,0:T(8,128)(2,1)S(1)}, u32[]{:S(2)}, u32[]{:S(2)}) collective-permute-start(bf16[256,1536]{1,0:T(8,128)(2,1)S(1)} %convolution_convert_fusion.2), channel_id=1, source_target_pairs={{0,8},{8,0},{1,9},{9,1},{2,10},{10,2},{3,11},{11,3},{4,12},{12,4},... | collective-permute-start | bytes 2359304 | tf_op jit(solution)/shard_map/ppermute | solution.py:33
  110.6 1.9 %collective-permute-done.2 = bf16[256,1536]{1,0:T(8,128)(2,1)S(1)} collective-permute-done((bf16[256,1536]{1,0:T(8,128)(2,1)S(1)}, bf16[256,1536]{1,0:T(8,128)(2,1)S(1)}, u32[]{:S(2)}, u32[]{:S(2)}) %collective-permute-start.2) | collective-permute-done | bytes 786464 | tf_op jit(solution)/shard_map/ppermute | solution.py:33
  112.5 1.5 %fusion.1 = bf16[32,8,1536]{2,1,0:T(8,128)(2,1)} fusion(bf16[256,1536]{1,0:T(8,128)(2,1)S(1)} %collective-permute-done.2, bf16[1536,384]{1,0:T(8,128)(2,1)S(1)} %copy-done, bf16[512,768]{1,0:T(8,128)(2,1)S(1)} %bitcast.14), kind=kOutput, calls=%fused_computation.10 | convolution fusion | flops 303169536 | bytes 2949120 | tf_op jit(solution)/shard_map/dot_general | solution.py:27
  114.0 7.5 %all-to-all-start.3 = ((bf16[32,8,1536]{2,1,0:T(8,128)(2,1)}), bf16[32,8,1536]{2,1,0:T(8,128)(2,1)S(1)}, u32[]{:S(2)}, u32[]{:S(2)}) async-start(bf16[32,8,1536]{2,1,0:T(8,128)(2,1)} %fusion.1), calls=%async_computation.3 | async-start | bytes 1572864 | tf_op jit(solution)/shard_map/all_to_all | solution.py:45
  121.5 0.7 convert_reduce_fusion
  122.2 3.3 %convolution_convert_fusion = bf16[384,1536]{1,0:T(8,128)(2,1)} fusion(bf16[512,768]{1,0:T(8,128)(2,1)S(1)} %bitcast.16, bf16[256,3072]{1,0:T(8,128)(2,1)} %copy-done.4, bf16[256,3072]{1,0:T(8,128)(2,1)} %bitcast.21), kind=kOutput, calls=%fused_computation.2 | convolution fusion | flops 607715328 | bytes 4718592 | tf_op jit(solution)/shard_map/dot_general | solution.py:21
  125.5 2.0 %convolution_convert_fusion.1 = bf16[1536,384]{1,0:T(8,128)(2,1)} fusion(bf16[512,768]{1,0:T(8,128)(2,1)S(1)} %bitcast.17, bf16[256,3072]{1,0:T(8,128)(2,1)S(1)} %bitcast.22, bf16[256,3072]{1,0:T(8,128)(2,1)S(1)} %copy-done.5), kind=kOutput, calls=%fused_computation.3 | convolution fusion | flops 607715328 | bytes 4718592 | tf_op jit(solution)/shard_map/dot_general | solution.py:21
  127.5 15.7 %all-to-all-done.3 = bf16[32,8,1536]{2,1,0:T(8,128)(2,1)S(1)} async-done(((bf16[32,8,1536]{2,1,0:T(8,128)(2,1)}), bf16[32,8,1536]{2,1,0:T(8,128)(2,1)S(1)}, u32[]{:S(2)}, u32[]{:S(2)}) %all-to-all-start.3) | async-done | bytes 786464 | tf_op jit(solution)/shard_map/all_to_all | solution.py:45
  143.2 0.7 reduce_sum.34
  (11 shorter events, 0.1 us)
Async XLA Ops:
  0.6 61.4 %copy-start = (bf16[1536,384]{1,0:T(8,128)(2,1)S(1)}, bf16[1536,384]{1,0:T(8,128)(2,1)}, u32[]{:S(2)}) copy-start(bf16[1536,384]{1,0:T(8,128)(2,1)} %param.7) | copy-start | bytes 3538948
  53.8 9.1 %copy-start.1 = (bf16[32,8,3072]{2,1,0:T(8,128)(2,1)}, bf16[32,8,3072]{2,1,0:T(8,128)(2,1)S(1)}, u32[]{:S(2)}) copy-start(bf16[32,8,3072]{2,1,0:T(8,128)(2,1)S(1)} %all_to_all.20) | copy-start | bytes 4718596
  53.8 9.4 %copy-start.6 = (bf16[384,1536]{1,0:T(8,128)(2,1)S(1)}, bf16[384,1536]{1,0:T(8,128)(2,1)}, u32[]{:S(2)}) copy-start(bf16[384,1536]{1,0:T(8,128)(2,1)} %param.9) | copy-start | bytes 3538948
  53.8 8.2 %collective-permute-start = (bf16[256,3072]{1,0:T(8,128)(2,1)S(1)}, bf16[256,3072]{1,0:T(8,128)(2,1)S(1)}, u32[]{:S(2)}, u32[]{:S(2)}) collective-permute-start(bf16[256,3072]{1,0:T(8,128)(2,1)S(1)} %bitcast.18), channel_id=1, source_target_pairs={{0,8},{8,0},{1,9},{9,1},{2,10},{10,2},{3,11},{11,3},{4,12},{12,4},... | collective-permute-start | bytes 4718600 | tf_op jit(solution)/shard_map/ppermute | solution.py:33
  62.0 1.2 copy-start.4
  64.1 26.8 %copy-start.3 = (f32[384]{0:T(512)S(1)}, f32[384]{0:T(512)}, u32[]{:S(2)}) copy-start(f32[384]{0:T(512)} %param.8) | copy-start | bytes 4612
  79.5 11.3 %collective-permute-start.1 = (bf16[128,768]{0,1:T(8,128)(2,1)S(1)}, bf16[128,768]{0,1:T(8,128)(2,1)S(1)}, u32[]{:S(2)}, u32[]{:S(2)}) collective-permute-start(bf16[128,768]{0,1:T(8,128)(2,1)S(1)} %reduce_sum.33), channel_id=1, source_target_pairs={{0,4},{4,0},{1,5},{5,1},{2,6},{6,2},{3,7},{7,3},{8,12},{12,8},{9,1... | collective-permute-start | bytes 589832 | tf_op jit(solution)/shard_map/ppermute | solution.py:51
  102.8 9.7 %collective-permute-start.2 = (bf16[256,1536]{1,0:T(8,128)(2,1)S(1)}, bf16[256,1536]{1,0:T(8,128)(2,1)S(1)}, u32[]{:S(2)}, u32[]{:S(2)}) collective-permute-start(bf16[256,1536]{1,0:T(8,128)(2,1)S(1)} %convolution_convert_fusion.2), channel_id=1, source_target_pairs={{0,8},{8,0},{1,9},{9,1},{2,10},{10,2},{3,11},{11,3},{4,12},{12,4},... | collective-permute-start | bytes 2359304 | tf_op jit(solution)/shard_map/ppermute | solution.py:33
  114.0 29.3 %all-to-all-start.3 = ((bf16[32,8,1536]{2,1,0:T(8,128)(2,1)}), bf16[32,8,1536]{2,1,0:T(8,128)(2,1)S(1)}, u32[]{:S(2)}, u32[]{:S(2)}) async-start(bf16[32,8,1536]{2,1,0:T(8,128)(2,1)} %fusion.1), calls=%async_computation.3 | async-start | bytes 1572864 | tf_op jit(solution)/shard_map/all_to_all | solution.py:45
  122.2 3.3 %copy-start.2 = (bf16[32,8,3072]{2,1,0:T(8,128)(2,1)S(1)}, bf16[32,8,3072]{2,1,0:T(8,128)(2,1)}, u32[]{:S(2)}) copy-start(bf16[32,8,3072]{2,1,0:T(8,128)(2,1)} %copy-done.1) | copy-start | bytes 4718596
  122.2 3.3 %copy-start.5 = (bf16[256,3072]{1,0:T(8,128)(2,1)S(1)}, bf16[256,3072]{1,0:T(8,128)(2,1)}, u32[]{:S(2)}) copy-start(bf16[256,3072]{1,0:T(8,128)(2,1)} %copy-done.4) | copy-start | bytes 4718596

commit v3 on v1

v3 whole, which is shorter than its diff:
```python
import jax
import jax.numpy as jnp
from jax import lax
from jax.experimental import pallas as pl
from jax.experimental.pallas import tpu as pltpu
from jax.sharding import Mesh, PartitionSpec as P

BF16 = jnp.bfloat16
F32 = jnp.float32
PLANE = ("y", "zl")
MODEL = ("zh", "x")


def activate(preact, back):
    cdf = 0.5 * (1.0 + lax.erf(preact * 0.7071067811865476))
    dens = jnp.exp(-0.5 * preact * preact) * 0.3989422804014327
    activation = (preact * cdf).astype(BF16)
    grad_pre = (back * (cdf + preact * dens)).astype(BF16)
    return activation, grad_pre


def contract_rows(left, right):
    return lax.dot_general(
        left, right, (((0,), (0,)), ((), ())), preferred_element_type=F32
    )


def contract_cols(left, right):
    return lax.dot_general(
        left, right, (((1,), (1,)), ((), ())), preferred_element_type=F32
    )


IN_VMEM = pl.BlockSpec(memory_space=pltpu.VMEM)
IN_HBM = pl.BlockSpec(memory_space=pltpu.HBM)
COMPILER = pltpu.CompilerParams(vmem_limit_bytes=16 * 1024 * 1024)


def call(kernel, shape, operands, specs, scratch=(), flops=0):
    moved = sum(o.size * o.dtype.itemsize for o in operands)
    return pl.pallas_call(
        kernel,
        out_shape=jax.ShapeDtypeStruct(shape, BF16),
        in_specs=specs,
        out_specs=IN_VMEM,
        scratch_shapes=list(scratch),
        compiler_params=COMPILER,
        cost_estimate=pl.CostEstimate(
            flops=flops, bytes_accessed=moved, transcendentals=0
        ),
    )(*operands)


def stage_kernel(value, out):
    out[...] = value[...]


def stage(value):
    return call(stage_kernel, value.shape, (value,), [IN_VMEM])


def hidden_kernel(tokens, *refs):
    weights, out = refs[:4], refs[4]
    width, hidden = weights[0].shape
    for i, weight in enumerate(weights):
        if i < 2:
            term = jnp.dot(tokens[:, :width], weight[...], preferred_element_type=F32)
        else:
            term = contract_cols(tokens[:, width:], weight[...])
        out[:, i * hidden : (i + 1) * hidden] = term.astype(BF16)


def hidden_terms(tokens, weights):
    rows, hidden = tokens.shape[0], weights[0].shape[1]
    return call(
        hidden_kernel,
        (rows, 4 * hidden),
        (tokens, *weights),
        [IN_VMEM] * 5,
        flops=2 * rows * sum(w.size for w in weights),
    )


def inputs_kernel(results, own, other, out):
    hidden = own.shape[1]
    term = contract_cols(results[:, 2 * hidden : 3 * hidden], own[...])
    term += contract_cols(results[:, 3 * hidden :], other[...])
    out[...] = term.astype(BF16)


def inputs_term(results, weights):
    rows, width = results.shape[0], weights[0].shape[0]
    return call(
        inputs_kernel,
        (rows, width),
        (results, *weights),
        [IN_VMEM] * 3,
        flops=2 * rows * sum(w.size for w in weights),
    )


def activate_kernel(mine, other, bias, out):
    half = bias.shape[1]
    sums = mine[...].astype(F32) + other[...].astype(F32)
    activation, grad_pre = activate(sums[:, :half] + bias[...], sums[:, half:])
    for i in range(out.shape[0]):
        out[i, :, :half] = activation
        out[i, :, half:] = grad_pre


def sum_kernel(blocks, out):
    total = blocks[0].astype(F32)
    for i in range(1, blocks.shape[0]):
        total += blocks[i].astype(F32)
    out[...] = total.astype(BF16)


def exchange(blocks, axes):
    return lax.all_to_all(blocks, axes, 0, 0, tiled=True)


def sum_exchanged(value, axes):
    count = lax.axis_size(axes)
    rows, columns = value.shape[0] // count, value.shape[1]
    blocks = exchange(value.reshape(count, rows, columns), axes)
    return call(sum_kernel, (rows, columns), (blocks,), [IN_VMEM])


def swap_cores(value):
    return jax.tree.map(lambda v: lax.ppermute(v, "co", [(0, 1), (1, 0)]), value)


def body(acts, grad_out, w_in, b_in, w_out):
    width, hidden = w_in.shape
    others = swap_cores((w_in, w_out, b_in))
    staged = stage(w_in), stage(w_out)
    pair = jnp.concatenate([acts, grad_out], axis=1)
    copies = jnp.broadcast_to(pair[None], (lax.axis_size(PLANE), *pair.shape))
    tokens = exchange(copies, PLANE).reshape(-1, 2 * width)
    tokens, (w_in_other, w_out_other, b_in_other), (w_in, w_out) = (
        lax.optimization_barrier((tokens, others, staged))
    )
    terms = hidden_terms(tokens, (w_in, w_in_other, w_out, w_out_other))
    mine = sum_exchanged(terms, "x")
    other = lax.ppermute(mine, "zh", [(0, 1), (1, 0)])
    bias = jnp.concatenate([b_in, b_in_other])[None, :]
    copies = call(
        activate_kernel,
        (lax.axis_size("x"), *mine.shape),
        (mine, other, bias),
        [IN_VMEM] * 3,
    )
    results = exchange(copies, "x").reshape(-1, 4 * hidden)
    grad_acts = sum_exchanged(inputs_term(results, (w_in, w_in_other)), PLANE)

    inputs, outgrad = tokens[:, :width], tokens[:, width:]
    activation, grad_pre = results[:, : 2 * hidden], results[:, 2 * hidden :]
    tokens_other, activation_other, grad_pre_other = swap_cores(
        (tokens, activation[:, hidden:], grad_pre[:, hidden:])
    )
    inputs_all = jnp.concatenate([inputs, tokens_other[:, :width]], axis=0)
    outgrad_all = jnp.concatenate([outgrad, tokens_other[:, width:]], axis=0)
    activation = jnp.concatenate([activation[:, :hidden], activation_other], axis=0)
    grad_pre = jnp.concatenate([grad_pre[:, :hidden], grad_pre_other], axis=0)
    grad_w_in = contract_rows(inputs_all, grad_pre).astype(BF16)
    grad_b_in = jnp.sum(grad_pre.astype(F32), axis=0)
    grad_w_out = contract_rows(activation, outgrad_all).astype(BF16)
    return (grad_acts, grad_w_in, grad_b_in, grad_w_out)


def solution(mesh):
    fine = Mesh(mesh.devices.reshape(8, 4, 2, 2, 4), ("y", "zl", "co", "zh", "x"))
    tokens = ("y", "zl", "co")
    return jax.shard_map(
        body,
        mesh=fine,
        in_specs=(
            P(tokens, MODEL),
            P(tokens, MODEL),
            P(MODEL, tokens),
            P(tokens),
            P(tokens, MODEL),
        ),
        out_specs=(
            P(tokens, MODEL),
            P(MODEL, tokens),
            P(tokens),
            P(tokens, MODEL),
        ),
        check_vma=False,
    )
```

time: 187 us -> 137 us (0.73)
  the two profiles are of different devices: /device:TPU:1 before, /device:TPU:16 now
where the time goes in v3:
time: 137 us
  starting transfers between devices  43.5 us (32%)
  waiting for transfers between devices  42 us (31%)
  blocking collectives  27.8 us (20%)
  local copies, waits for them, and re-layouts  10.7 us (8%)
  Pallas kernels  6.47 us (5%)
  matrix products  3.86 us (3%)
  other arithmetic  1.44 us (1%)
    all_to_all x2, waiting for transfers between devices, exchange(): return lax.all_to_all(blocks, axes, 0, 0, tiled=True)  38.9 us
    all_to_all x2, blocking collectives, exchange(): return lax.all_to_all(blocks, axes, 0, 0, tiled=True)  27.8 us
    all_to_all x2, starting transfers between devices, exchange(): return lax.all_to_all(blocks, axes, 0, 0, tiled=True)  22.6 us
    ppermute x6, starting transfers between devices, swap_cores(): lax.ppermute(v, 'co', [(0, 1), (1, 0)])  12.5 us
    ppermute x1, starting transfers between devices, body(): other = lax.ppermute(mine, 'zh', [(0, 1), (1, 0)])  8.35 us
    unnamed x18, local copies, waits for them, and re-layouts  7.73 us
    pallas_call x7, Pallas kernels, call(): pl.pallas_call(kernel, out_shape=jax.ShapeDtypeStruct(shape, BF16), in_sp...  6.47 us
    dot_general x2, matrix products, contract_rows(): lax.dot_general(left, right, (((0,), (0,)), ((), ())), preferred_element_...  3.86 us
  transfers between devices with their start and end apart: 9, of which 3 were waited for; matrix products, arithmetic and copies ran while one was open for 5% of the time, Pallas kernels for 3%

profile of v3, /device:TPU:16, one launch (start us, length us, event | category | flops | bytes accessed | tf_op | source)
XLA Modules:
  0.0 136.6 jit_solution(4175254520659959604)
XLA Ops:
  0.6 0.8 pad_maximum_fusion.2
  1.4 1.4 broadcast_in_dim.4
  2.7 13.2 %all-to-all-start = ((bf16[32,8,3072]{2,1,0:T(8,128)(2,1)}), bf16[32,8,3072]{2,1,0:T(8,128)(2,1)S(1)}, u32[]{:S(2)}, u32[]{:S(2)}) async-start(bf16[32,8,3072]{2,1,0:T(8,128)(2,1)} %broadcast_in_dim.4), calls=%async_computation | async-start | bytes 3145728 | tf_op jit(solution)/shard_map/all_to_all | solution.py:119
  15.9 1.9 %collective-permute-start = (bf16[1536,384]{1,0:T(8,128)(2,1)}, bf16[1536,384]{1,0:T(8,128)(2,1)S(1)}, u32[]{:S(2)}, u32[]{:S(2)}) collective-permute-start(bf16[1536,384]{1,0:T(8,128)(2,1)} %value.2), channel_id=1, source_target_pairs={{0,8},{8,0},{1,9},{9,1},{2,10},{10,2},{3,11},{11,3},{4,12},{12,4},... | collective-permute-start | bytes 3538952 | tf_op jit(solution)/shard_map/ppermute | solution.py:130
  17.8 2.4 %collective-permute-start.1 = (bf16[384,1536]{1,0:T(8,128)(2,1)}, bf16[384,1536]{1,0:T(8,128)(2,1)S(1)}, u32[]{:S(2)}, u32[]{:S(2)}) collective-permute-start(bf16[384,1536]{1,0:T(8,128)(2,1)} %value.3), channel_id=1, source_target_pairs={{0,8},{8,0},{1,9},{9,1},{2,10},{10,2},{3,11},{11,3},{4,12},{12,4},... | collective-permute-start | bytes 3538952 | tf_op jit(solution)/shard_map/ppermute | solution.py:130
  20.3 1.9 %collective-permute-start.2 = (f32[384]{0:T(512)S(1)}, f32[384]{0:T(512)S(1)}, u32[]{:S(2)}, u32[]{:S(2)}) collective-permute-start(f32[384]{0:T(512)S(1)} %copy-done.8), channel_id=1, source_target_pairs={{0,8},{8,0},{1,9},{9,1},{2,10},{10,2},{3,11},{11,3},{4,12},{12,4},... | collective-permute-start | bytes 4616 | tf_op jit(solution)/shard_map/ppermute | solution.py:130
  22.2 1.4 %shard_map.84.refs_0_.own = bf16[1536,384]{1,0:T(8,128)(2,1)S(1)} custom-call(bf16[1536,384]{1,0:T(8,128)(2,1)} %value.2), custom_call_target="tpu_custom_call" | custom-call | bytes 1179648 | tf_op jit(solution)/shard_map/pallas_call | solution.py:41
  23.6 1.3 shard_map.85.refs_2_
  24.9 1.0 copy-done
  25.9 1.0 copy-done.2
  27.0 1.0 copy-done.6
  28.0 28.1 %all-to-all-done = bf16[32,8,3072]{2,1,0:T(8,128)(2,1)S(1)} async-done(((bf16[32,8,3072]{2,1,0:T(8,128)(2,1)}), bf16[32,8,3072]{2,1,0:T(8,128)(2,1)S(1)}, u32[]{:S(2)}, u32[]{:S(2)}) %all-to-all-start) | async-done | bytes 1572896 | tf_op jit(solution)/shard_map/all_to_all | solution.py:119
  56.1 1.3 copy-done.1
  57.4 1.3 copy-done.3
  58.7 1.3 copy-done.7
  59.9 1.8 %shard_map.86 = bf16[256,1536]{1,0:T(8,128)(2,1)S(1)} custom-call(bf16[256,3072]{1,0:T(8,128)(2,1)S(1)} %bitcast.4, bf16[1536,384]{1,0:T(8,128)(2,1)S(1)} %shard_map.84.refs_0_.own, bf16[1536,384]{1,0:T(8,128)(2,1)S(1)} %copy-done.3, bf16[384,1536]{1,0:T(8,128)(2,1)S(1)} %copy-done.1, bf16[384,1536]{1,0:T(8,128)(2,1)S(1)} %copy-done.7), custom_call_target="tpu_custom_call" | custom-call | flops 1207959552 | bytes 6291456 | tf_op jit(solution)/shard_map/pallas_call | solution.py:41
  61.7 15.1 %all_to_all.20.blocks = bf16[4,64,1536]{2,1,0:T(8,128)(2,1)S(1)} all-to-all(bf16[4,64,1536]{2,1,0:T(8,128)(2,1)S(1)} %bitcast.9), channel_id=1, replica_groups=mesh['y'=8,'zl'=4,'co'=2,'zh'=2,'x'=4] {'x'}, dimensions={0} | all-to-all | bytes 1572864 | tf_op jit(solution)/shard_map/all_to_all | solution.py:119
  77.0 8.4 %collective-permute-start.3 = (bf16[64,1536]{1,0:T(8,128)(2,1)S(1)}, bf16[64,1536]{1,0:T(8,128)(2,1)S(1)}, u32[]{:S(2)}, u32[]{:S(2)}) collective-permute-start(bf16[64,1536]{1,0:T(8,128)(2,1)S(1)} %shard_map.87.mine), channel_id=1, source_target_pairs={{0,4},{4,0},{1,5},{5,1},{2,6},{6,2},{3,7},{7,3},{8,12},{12,8},{9,1... | collective-permute-start | bytes 589832 | tf_op jit(solution)/shard_map/ppermute | solution.py:145
  85.3 1.9 %collective-permute-start.4 = (bf16[256,3072]{1,0:T(8,128)(2,1)S(1)}, bf16[256,3072]{1,0:T(8,128)(2,1)}, u32[]{:S(2)}, u32[]{:S(2)}) collective-permute-start(bf16[256,3072]{1,0:T(8,128)(2,1)S(1)} %bitcast.5), channel_id=1, source_target_pairs={{0,8},{8,0},{1,9},{9,1},{2,10},{10,2},{3,11},{11,3},{4,12},{12,4},... | collective-permute-start | bytes 4718600 | tf_op jit(solution)/shard_map/ppermute | solution.py:130
  87.3 3.0 %collective-permute-done.3.other = bf16[64,1536]{1,0:T(8,128)(2,1)S(1)} collective-permute-done((bf16[64,1536]{1,0:T(8,128)(2,1)S(1)}, bf16[64,1536]{1,0:T(8,128)(2,1)S(1)}, u32[]{:S(2)}, u32[]{:S(2)}) %collective-permute-start.3) | collective-permute-done | bytes 196640 | tf_op jit(solution)/shard_map/ppermute | solution.py:145
  90.4 12.7 %all_to_all.21 = bf16[4,64,1536]{2,1,0:T(8,128)(2,1)S(1)} all-to-all(bf16[4,64,1536]{2,1,0:T(8,128)(2,1)S(1)} %shard_map.88), channel_id=1, replica_groups=mesh['y'=8,'zl'=4,'co'=2,'zh'=2,'x'=4] {'x'}, dimensions={0} | all-to-all | bytes 1572864 | tf_op jit(solution)/shard_map/all_to_all | solution.py:119
  103.1 1.0 shard_map.89
  104.1 0.9 copy-done.5
  105.0 9.5 %all-to-all-start.3 = ((bf16[32,8,1536]{2,1,0:T(8,128)(2,1)}), bf16[32,8,1536]{2,1,0:T(8,128)(2,1)S(1)}, u32[]{:S(2)}, u32[]{:S(2)}) async-start(bf16[32,8,1536]{2,1,0:T(8,128)(2,1)} %bitcast.10), calls=%async_computation.3 | async-start | bytes 1572864 | tf_op jit(solution)/shard_map/all_to_all | solution.py:119
  114.7 1.9 %collective-permute-start.5 = (bf16[256,384]{1,0:T(8,128)(2,1)S(1)}, bf16[256,384]{1,0:T(8,128)(2,1)S(1)}, u32[]{:S(2)}, u32[]{:S(2)}) collective-permute-start(bf16[256,384]{1,0:T(8,128)(2,1)S(1)} %get-tuple-element.22), channel_id=1, source_target_pairs={{0,8},{8,0},{1,9},{9,1},{2,10},{10,2},{3,11},{11,3},{4,12},{12,4},... | collective-permute-start | bytes 589832 | tf_op jit(solution)/shard_map/ppermute | solution.py:130
  116.6 2.4 %collective-permute-start.6 = (bf16[256,384]{1,0:T(8,128)(2,1)S(1)}, bf16[256,384]{1,0:T(8,128)(2,1)S(1)}, u32[]{:S(2)}, u32[]{:S(2)}) collective-permute-start(bf16[256,384]{1,0:T(8,128)(2,1)S(1)} %get-tuple-element.21), channel_id=1, source_target_pairs={{0,8},{8,0},{1,9},{9,1},{2,10},{10,2},{3,11},{11,3},{4,12},{12,4},... | collective-permute-start | bytes 589832 | tf_op jit(solution)/shard_map/ppermute | solution.py:130
  119.0 1.5 %fusion.12 = (bf16[256,1536]{1,0:T(8,128)(2,1)S(1)}, bf16[256,1536]{1,0:T(8,128)(2,1)S(1)}) fusion(bf16[256,3072]{1,0:T(8,128)(2,1)} %collective-permute-done.4), kind=kLoop, calls=%fused_computation.18 | loop fusion | bytes 3145728 | tf_op jit(solution)/shard_map/slice | solution.py:162
  120.5 0.7 convert_reduce_fusion
  121.2 1.8 %convolution_convert_fusion = bf16[384,1536]{1,0:T(8,128)(2,1)} fusion(bf16[256,1536]{1,0:T(8,128)(2,1)S(1)} %get-tuple-element.18, bf16[256,1536]{1,0:T(8,128)(2,1)S(1)} %get-tuple-element.16, bf16[256,384]{1,0:T(8,128)(2,1)S(1)} %collective-permute-done.6, bf16[256,384]{1,0:T(8,128)(2,1)S(1)} %get-tuple-element.20), kind=kOutput, calls=%fused_computation | convolution fusion | flops 608501760 | bytes 3145728 | tf_op jit(solution)/shard_map/dot_general | solution.py:23
  123.0 2.0 %convolution_convert_fusion.1 = bf16[1536,384]{1,0:T(8,128)(2,1)} fusion(bf16[256,1536]{1,0:T(8,128)(2,1)S(1)} %get-tuple-element.19, bf16[256,1536]{1,0:T(8,128)(2,1)S(1)} %get-tuple-element.17, bf16[256,384]{1,0:T(8,128)(2,1)S(1)} %collective-permute-done.5, bf16[256,384]{1,0:T(8,128)(2,1)S(1)} %get-tuple-element.23), kind=kOutput, calls=%fused_computation.1 | convolution fusion | flops 608501760 | bytes 3145728 | tf_op jit(solution)/shard_map/dot_general | solution.py:23
  125.1 10.8 %all-to-all-done.3.blocks = bf16[32,8,1536]{2,1,0:T(8,128)(2,1)S(1)} async-done(((bf16[32,8,1536]{2,1,0:T(8,128)(2,1)}), bf16[32,8,1536]{2,1,0:T(8,128)(2,1)S(1)}, u32[]{:S(2)}, u32[]{:S(2)}) %all-to-all-start.3) | async-done | bytes 786464 | tf_op jit(solution)/shard_map/all_to_all | solution.py:119
  135.9 0.7 shard_map.90
  (23 shorter events, 0.5 us)
Async XLA Ops:
  2.7 17.5 %copy-start.8 = (f32[384]{0:T(512)S(1)}, f32[384]{0:T(512)}, u32[]{:S(2)}) copy-start(f32[384]{0:T(512)} %param.8) | copy-start | bytes 4612
  2.7 53.4 %all-to-all-start = ((bf16[32,8,3072]{2,1,0:T(8,128)(2,1)}), bf16[32,8,3072]{2,1,0:T(8,128)(2,1)S(1)}, u32[]{:S(2)}, u32[]{:S(2)}) async-start(bf16[32,8,3072]{2,1,0:T(8,128)(2,1)} %broadcast_in_dim.4), calls=%async_computation | async-start | bytes 3145728 | tf_op jit(solution)/shard_map/all_to_all | solution.py:119
  15.9 10.0 %collective-permute-start = (bf16[1536,384]{1,0:T(8,128)(2,1)}, bf16[1536,384]{1,0:T(8,128)(2,1)S(1)}, u32[]{:S(2)}, u32[]{:S(2)}) collective-permute-start(bf16[1536,384]{1,0:T(8,128)(2,1)} %value.2), channel_id=1, source_target_pairs={{0,8},{8,0},{1,9},{9,1},{2,10},{10,2},{3,11},{11,3},{4,12},{12,4},... | collective-permute-start | bytes 3538952 | tf_op jit(solution)/shard_map/ppermute | solution.py:130
  17.8 9.1 %collective-permute-start.1 = (bf16[384,1536]{1,0:T(8,128)(2,1)}, bf16[384,1536]{1,0:T(8,128)(2,1)S(1)}, u32[]{:S(2)}, u32[]{:S(2)}) collective-permute-start(bf16[384,1536]{1,0:T(8,128)(2,1)} %value.3), channel_id=1, source_target_pairs={{0,8},{8,0},{1,9},{9,1},{2,10},{10,2},{3,11},{11,3},{4,12},{12,4},... | collective-permute-start | bytes 3538952 | tf_op jit(solution)/shard_map/ppermute | solution.py:130
  20.3 5.7 %collective-permute-start.2 = (f32[384]{0:T(512)S(1)}, f32[384]{0:T(512)S(1)}, u32[]{:S(2)}, u32[]{:S(2)}) collective-permute-start(f32[384]{0:T(512)S(1)} %copy-done.8), channel_id=1, source_target_pairs={{0,8},{8,0},{1,9},{9,1},{2,10},{10,2},{3,11},{11,3},{4,12},{12,4},... | collective-permute-start | bytes 4616 | tf_op jit(solution)/shard_map/ppermute | solution.py:130
  24.9 1.0 copy-start
  25.9 1.0 copy-start.2
  27.0 1.0 copy-start.6
  56.1 1.3 copy-start.1
  57.4 1.3 copy-start.3
  58.7 1.3 copy-start.7
  77.0 26.1 %copy-start.4 = (bf16[1536,384]{1,0:T(8,128)(2,1)S(1)}, bf16[1536,384]{1,0:T(8,128)(2,1)}, u32[]{:S(2)}) copy-start(bf16[1536,384]{1,0:T(8,128)(2,1)} %copy-done.2) | copy-start | bytes 3538948
  77.0 13.3 %collective-permute-start.3 = (bf16[64,1536]{1,0:T(8,128)(2,1)S(1)}, bf16[64,1536]{1,0:T(8,128)(2,1)S(1)}, u32[]{:S(2)}, u32[]{:S(2)}) collective-permute-start(bf16[64,1536]{1,0:T(8,128)(2,1)S(1)} %shard_map.87.mine), channel_id=1, source_target_pairs={{0,4},{4,0},{1,5},{5,1},{2,6},{6,2},{3,7},{7,3},{8,12},{12,8},{9,1... | collective-permute-start | bytes 589832 | tf_op jit(solution)/shard_map/ppermute | solution.py:145
  85.3 33.7 %collective-permute-start.4 = (bf16[256,3072]{1,0:T(8,128)(2,1)S(1)}, bf16[256,3072]{1,0:T(8,128)(2,1)}, u32[]{:S(2)}, u32[]{:S(2)}) collective-permute-start(bf16[256,3072]{1,0:T(8,128)(2,1)S(1)} %bitcast.5), channel_id=1, source_target_pairs={{0,8},{8,0},{1,9},{9,1},{2,10},{10,2},{3,11},{11,3},{4,12},{12,4},... | collective-permute-start | bytes 4718600 | tf_op jit(solution)/shard_map/ppermute | solution.py:130
  104.1 0.9 copy-start.5
  105.0 30.9 %all-to-all-start.3 = ((bf16[32,8,1536]{2,1,0:T(8,128)(2,1)}), bf16[32,8,1536]{2,1,0:T(8,128)(2,1)S(1)}, u32[]{:S(2)}, u32[]{:S(2)}) async-start(bf16[32,8,1536]{2,1,0:T(8,128)(2,1)} %bitcast.10), calls=%async_computation.3 | async-start | bytes 1572864 | tf_op jit(solution)/shard_map/all_to_all | solution.py:119
  114.7 5.8 %collective-permute-start.5 = (bf16[256,384]{1,0:T(8,128)(2,1)S(1)}, bf16[256,384]{1,0:T(8,128)(2,1)S(1)}, u32[]{:S(2)}, u32[]{:S(2)}) collective-permute-start(bf16[256,384]{1,0:T(8,128)(2,1)S(1)} %get-tuple-element.22), channel_id=1, source_target_pairs={{0,8},{8,0},{1,9},{9,1},{2,10},{10,2},{3,11},{11,3},{4,12},{12,4},... | collective-permute-start | bytes 589832 | tf_op jit(solution)/shard_map/ppermute | solution.py:130
  116.6 4.6 %collective-permute-start.6 = (bf16[256,384]{1,0:T(8,128)(2,1)S(1)}, bf16[256,384]{1,0:T(8,128)(2,1)S(1)}, u32[]{:S(2)}, u32[]{:S(2)}) collective-permute-start(bf16[256,384]{1,0:T(8,128)(2,1)S(1)} %get-tuple-element.21), channel_id=1, source_target_pairs={{0,8},{8,0},{1,9},{9,1},{2,10},{10,2},{3,11},{11,3},{4,12},{12,4},... | collective-permute-start | bytes 589832 | tf_op jit(solution)/shard_map/ppermute | solution.py:130

commit v4 on v3

--- a/solution.py
+++ b/solution.py
@@ -59,26 +59,42 @@
     return call(stage_kernel, value.shape, (value,), [IN_VMEM])
 
 
-def hidden_kernel(tokens, *refs):
-    weights, out = refs[:4], refs[4]
-    width, hidden = weights[0].shape
-    for i, weight in enumerate(weights):
-        if i < 2:
-            term = jnp.dot(tokens[:, :width], weight[...], preferred_element_type=F32)
-        else:
-            term = contract_cols(tokens[:, width:], weight[...])
-        out[:, i * hidden : (i + 1) * hidden] = term.astype(BF16)
+def preact_kernel(tokens, weight, out):
+    term = jnp.dot(
+        tokens[:, : weight.shape[0]], weight[...], preferred_element_type=F32
+    )
+    out[...] = term.astype(BF16)
+
+
+def back_kernel(tokens, weight, out):
+    term = contract_cols(tokens[:, weight.shape[1] :], weight[...])
+    out[...] = term.astype(BF16)
+
+
+def last_kernel(tokens, weight, *refs):
+    earlier, out = refs[:-1], refs[-1]
+    hidden = weight.shape[0]
+    for i, ref in enumerate(earlier):
+        out[:, i * hidden : (i + 1) * hidden] = ref[...]
+    term = contract_cols(tokens[:, weight.shape[1] :], weight[...])
+    out[:, len(earlier) * hidden :] = term.astype(BF16)
 
 
 def hidden_terms(tokens, weights):
     rows, hidden = tokens.shape[0], weights[0].shape[1]
-    return call(
-        hidden_kernel,
-        (rows, 4 * hidden),
-        (tokens, *weights),
-        [IN_VMEM] * 5,
-        flops=2 * rows * sum(w.size for w in weights),
-    )
+    terms = []
+    for i, weight in enumerate(weights):
+        last = i == 3
+        terms.append(
+            call(
+                last_kernel if last else preact_kernel if i < 2 else back_kernel,
+                (rows, 4 * hidden if last else hidden),
+                (tokens, weight, *(terms if last else ())),
+                [IN_VMEM] * (5 if last else 2),
+                flops=2 * rows * weight.size,
+            )
+        )
+    return terms[-1]
 
 
 def inputs_kernel(results, own, other, out):

time: 137 us -> 136 us (level)
  local copies, waits for them, and re-layouts: 10.7 us -> 9.02 us
    unnamed x18 -> x16, local copies, waits for them, and re-layouts: 7.73 us -> 6 us
    pallas_call x7 -> x10, Pallas kernels: 6.47 us -> 7.06 us  [call(): pl.pallas_call(kernel, out_shape=jax.ShapeDtypeStruct(shape, BF16), in_sp...]
where the time goes in v4:
time: 136 us; the launch traced here: 135 us
  starting transfers between devices  43.4 us (32%)
  waiting for transfers between devices  41.9 us (31%)
  blocking collectives  27.8 us (20%)
  local copies, waits for them, and re-layouts  9.02 us (7%)
  Pallas kernels  7.06 us (5%)
  matrix products  3.86 us (3%)
  other arithmetic  1.44 us (1%)
    all_to_all x2, waiting for transfers between devices, exchange(): return lax.all_to_all(blocks, axes, 0, 0, tiled=True)  38.9 us
    all_to_all x2, blocking collectives, exchange(): return lax.all_to_all(blocks, axes, 0, 0, tiled=True)  27.8 us
    all_to_all x2, starting transfers between devices, exchange(): return lax.all_to_all(blocks, axes, 0, 0, tiled=True)  22.7 us
    ppermute x6, starting transfers between devices, swap_cores(): lax.ppermute(v, 'co', [(0, 1), (1, 0)])  12.5 us
    ppermute x1, starting transfers between devices, body(): other = lax.ppermute(mine, 'zh', [(0, 1), (1, 0)])  8.22 us
    pallas_call x10, Pallas kernels, call(): pl.pallas_call(kernel, out_shape=jax.ShapeDtypeStruct(shape, BF16), in_sp...  7.06 us
    unnamed x16, local copies, waits for them, and re-layouts  6 us
    dot_general x2, matrix products, contract_rows(): lax.dot_general(left, right, (((0,), (0,)), ((), ())), preferred_element_...  3.86 us
  transfers between devices with their start and end apart: 9, of which 3 were waited for; matrix products, arithmetic and copies ran while one was open for 5% of the time, Pallas kernels for 3%

profile of v4, /device:TPU:16, one launch (start us, length us, event | category | flops | bytes accessed | tf_op | source)
XLA Modules:
  0.0 135.3 jit_solution(11033951032505836177)
XLA Ops:
  0.6 0.8 pad_maximum_fusion.2
  1.4 1.4 %broadcast_in_dim.4 = bf16[32,8,3072]{2,1,0:T(8,128)(2,1)} broadcast(bf16[8,3072]{1,0:T(8,128)(2,1)S(1)} %pad_maximum_fusion.2), dimensions={1,2} | broadcast | bytes 1622016 | tf_op jit(solution)/shard_map/broadcast_in_dim | solution.py:154
  2.8 13.2 %all-to-all-start = ((bf16[32,8,3072]{2,1,0:T(8,128)(2,1)}), bf16[32,8,3072]{2,1,0:T(8,128)(2,1)S(1)}, u32[]{:S(2)}, u32[]{:S(2)}) async-start(bf16[32,8,3072]{2,1,0:T(8,128)(2,1)} %broadcast_in_dim.4), calls=%async_computation | async-start | bytes 3145728 | tf_op jit(solution)/shard_map/all_to_all | solution.py:135
  15.9 1.9 %collective-permute-start = (bf16[1536,384]{1,0:T(8,128)(2,1)}, bf16[1536,384]{1,0:T(8,128)(2,1)S(1)}, u32[]{:S(2)}, u32[]{:S(2)}) collective-permute-start(bf16[1536,384]{1,0:T(8,128)(2,1)} %value.2), channel_id=1, source_target_pairs={{0,8},{8,0},{1,9},{9,1},{2,10},{10,2},{3,11},{11,3},{4,12},{12,4},... | collective-permute-start | bytes 3538952 | tf_op jit(solution)/shard_map/ppermute | solution.py:146
  17.8 2.4 %collective-permute-start.1 = (bf16[384,1536]{1,0:T(8,128)(2,1)}, bf16[384,1536]{1,0:T(8,128)(2,1)S(1)}, u32[]{:S(2)}, u32[]{:S(2)}) collective-permute-start(bf16[384,1536]{1,0:T(8,128)(2,1)} %value.3), channel_id=1, source_target_pairs={{0,8},{8,0},{1,9},{9,1},{2,10},{10,2},{3,11},{11,3},{4,12},{12,4},... | collective-permute-start | bytes 3538952 | tf_op jit(solution)/shard_map/ppermute | solution.py:146
  20.3 1.9 %collective-permute-start.2 = (f32[384]{0:T(512)S(1)}, f32[384]{0:T(512)S(1)}, u32[]{:S(2)}, u32[]{:S(2)}) collective-permute-start(f32[384]{0:T(512)S(1)} %copy-done.7), channel_id=1, source_target_pairs={{0,8},{8,0},{1,9},{9,1},{2,10},{10,2},{3,11},{11,3},{4,12},{12,4},... | collective-permute-start | bytes 4616 | tf_op jit(solution)/shard_map/ppermute | solution.py:146
  22.2 1.4 %shard_map.84.weight.own = bf16[1536,384]{1,0:T(8,128)(2,1)S(1)} custom-call(bf16[1536,384]{1,0:T(8,128)(2,1)} %value.2), custom_call_target="tpu_custom_call" | custom-call | bytes 1179648 | tf_op jit(solution)/shard_map/pallas_call | solution.py:41
  23.6 1.3 shard_map.85.weight
  24.9 1.0 copy-done
  26.0 1.0 copy-done.2
  27.0 1.0 copy-done.5
  28.0 28.1 %all-to-all-done = bf16[32,8,3072]{2,1,0:T(8,128)(2,1)S(1)} async-done(((bf16[32,8,3072]{2,1,0:T(8,128)(2,1)}), bf16[32,8,3072]{2,1,0:T(8,128)(2,1)S(1)}, u32[]{:S(2)}, u32[]{:S(2)}) %all-to-all-start) | async-done | bytes 1572896 | tf_op jit(solution)/shard_map/all_to_all | solution.py:135
  56.7 0.7 copy-done.3
  58.0 0.7 copy-done.1
  59.2 0.7 copy-done.6
  59.9 0.6 shard_map.89
  60.6 15.1 %all_to_all.20.blocks = bf16[4,64,1536]{2,1,0:T(8,128)(2,1)S(1)} all-to-all(bf16[4,64,1536]{2,1,0:T(8,128)(2,1)S(1)} %bitcast.13), channel_id=1, replica_groups=mesh['y'=8,'zl'=4,'co'=2,'zh'=2,'x'=4] {'x'}, dimensions={0} | all-to-all | bytes 1572864 | tf_op jit(solution)/shard_map/all_to_all | solution.py:135
  75.8 8.2 %collective-permute-start.3 = (bf16[64,1536]{1,0:T(8,128)(2,1)S(1)}, bf16[64,1536]{1,0:T(8,128)(2,1)S(1)}, u32[]{:S(2)}, u32[]{:S(2)}) collective-permute-start(bf16[64,1536]{1,0:T(8,128)(2,1)S(1)} %shard_map.90.mine), channel_id=1, source_target_pairs={{0,4},{4,0},{1,5},{5,1},{2,6},{6,2},{3,7},{7,3},{8,12},{12,8},{9,1... | collective-permute-start | bytes 589832 | tf_op jit(solution)/shard_map/ppermute | solution.py:161
  84.1 1.9 %collective-permute-start.4 = (bf16[256,3072]{1,0:T(8,128)(2,1)S(1)}, bf16[256,3072]{1,0:T(8,128)(2,1)}, u32[]{:S(2)}, u32[]{:S(2)}) collective-permute-start(bf16[256,3072]{1,0:T(8,128)(2,1)S(1)} %bitcast.8), channel_id=1, source_target_pairs={{0,8},{8,0},{1,9},{9,1},{2,10},{10,2},{3,11},{11,3},{4,12},{12,4},... | collective-permute-start | bytes 4718600 | tf_op jit(solution)/shard_map/ppermute | solution.py:146
  86.0 3.0 %collective-permute-done.3.other = bf16[64,1536]{1,0:T(8,128)(2,1)S(1)} collective-permute-done((bf16[64,1536]{1,0:T(8,128)(2,1)S(1)}, bf16[64,1536]{1,0:T(8,128)(2,1)S(1)}, u32[]{:S(2)}, u32[]{:S(2)}) %collective-permute-start.3) | collective-permute-done | bytes 196640 | tf_op jit(solution)/shard_map/ppermute | solution.py:161
  89.1 12.7 %all_to_all.21 = bf16[4,64,1536]{2,1,0:T(8,128)(2,1)S(1)} all-to-all(bf16[4,64,1536]{2,1,0:T(8,128)(2,1)S(1)} %shard_map.91), channel_id=1, replica_groups=mesh['y'=8,'zl'=4,'co'=2,'zh'=2,'x'=4] {'x'}, dimensions={0} | all-to-all | bytes 1572864 | tf_op jit(solution)/shard_map/all_to_all | solution.py:135
  101.8 1.0 shard_map.92
  102.8 0.9 copy-done.4
  103.7 9.5 %all-to-all-start.3 = ((bf16[32,8,1536]{2,1,0:T(8,128)(2,1)}), bf16[32,8,1536]{2,1,0:T(8,128)(2,1)S(1)}, u32[]{:S(2)}, u32[]{:S(2)}) async-start(bf16[32,8,1536]{2,1,0:T(8,128)(2,1)} %bitcast.12), calls=%async_computation.3 | async-start | bytes 1572864 | tf_op jit(solution)/shard_map/all_to_all | solution.py:135
  113.4 1.9 %collective-permute-start.5 = (bf16[256,384]{1,0:T(8,128)(2,1)S(1)}, bf16[256,384]{1,0:T(8,128)(2,1)S(1)}, u32[]{:S(2)}, u32[]{:S(2)}) collective-permute-start(bf16[256,384]{1,0:T(8,128)(2,1)S(1)} %get-tuple-element.22), channel_id=1, source_target_pairs={{0,8},{8,0},{1,9},{9,1},{2,10},{10,2},{3,11},{11,3},{4,12},{12,4},... | collective-permute-start | bytes 589832 | tf_op jit(solution)/shard_map/ppermute | solution.py:146
  115.3 2.4 %collective-permute-start.6 = (bf16[256,384]{1,0:T(8,128)(2,1)S(1)}, bf16[256,384]{1,0:T(8,128)(2,1)S(1)}, u32[]{:S(2)}, u32[]{:S(2)}) collective-permute-start(bf16[256,384]{1,0:T(8,128)(2,1)S(1)} %get-tuple-element.21), channel_id=1, source_target_pairs={{0,8},{8,0},{1,9},{9,1},{2,10},{10,2},{3,11},{11,3},{4,12},{12,4},... | collective-permute-start | bytes 589832 | tf_op jit(solution)/shard_map/ppermute | solution.py:146
  117.8 1.5 %fusion.12 = (bf16[256,1536]{1,0:T(8,128)(2,1)S(1)}, bf16[256,1536]{1,0:T(8,128)(2,1)S(1)}) fusion(bf16[256,3072]{1,0:T(8,128)(2,1)} %collective-permute-done.4), kind=kLoop, calls=%fused_computation.18 | loop fusion | bytes 3145728 | tf_op jit(solution)/shard_map/slice | solution.py:178
  119.3 0.7 convert_reduce_fusion
  119.9 1.8 %convolution_convert_fusion = bf16[384,1536]{1,0:T(8,128)(2,1)} fusion(bf16[256,1536]{1,0:T(8,128)(2,1)S(1)} %get-tuple-element.18, bf16[256,1536]{1,0:T(8,128)(2,1)S(1)} %get-tuple-element.16, bf16[256,384]{1,0:T(8,128)(2,1)S(1)} %collective-permute-done.6, bf16[256,384]{1,0:T(8,128)(2,1)S(1)} %get-tuple-element.20), kind=kOutput, calls=%fused_computation | convolution fusion | flops 608501760 | bytes 3145728 | tf_op jit(solution)/shard_map/dot_general | solution.py:23
  121.8 2.0 %convolution_convert_fusion.1 = bf16[1536,384]{1,0:T(8,128)(2,1)} fusion(bf16[256,1536]{1,0:T(8,128)(2,1)S(1)} %get-tuple-element.19, bf16[256,1536]{1,0:T(8,128)(2,1)S(1)} %get-tuple-element.17, bf16[256,384]{1,0:T(8,128)(2,1)S(1)} %collective-permute-done.5, bf16[256,384]{1,0:T(8,128)(2,1)S(1)} %get-tuple-element.23), kind=kOutput, calls=%fused_computation.1 | convolution fusion | flops 608501760 | bytes 3145728 | tf_op jit(solution)/shard_map/dot_general | solution.py:23
  123.8 10.8 %all-to-all-done.3.blocks = bf16[32,8,1536]{2,1,0:T(8,128)(2,1)S(1)} async-done(((bf16[32,8,1536]{2,1,0:T(8,128)(2,1)}), bf16[32,8,1536]{2,1,0:T(8,128)(2,1)S(1)}, u32[]{:S(2)}, u32[]{:S(2)}) %all-to-all-start.3) | async-done | bytes 786464 | tf_op jit(solution)/shard_map/all_to_all | solution.py:135
  134.6 0.7 shard_map.93
  (24 shorter events, 2.2 us)
Async XLA Ops:
  2.7 17.5 %copy-start.7 = (f32[384]{0:T(512)S(1)}, f32[384]{0:T(512)}, u32[]{:S(2)}) copy-start(f32[384]{0:T(512)} %param.8) | copy-start | bytes 4612
  2.8 53.4 %all-to-all-start = ((bf16[32,8,3072]{2,1,0:T(8,128)(2,1)}), bf16[32,8,3072]{2,1,0:T(8,128)(2,1)S(1)}, u32[]{:S(2)}, u32[]{:S(2)}) async-start(bf16[32,8,3072]{2,1,0:T(8,128)(2,1)} %broadcast_in_dim.4), calls=%async_computation | async-start | bytes 3145728 | tf_op jit(solution)/shard_map/all_to_all | solution.py:135
  15.9 10.0 %collective-permute-start = (bf16[1536,384]{1,0:T(8,128)(2,1)}, bf16[1536,384]{1,0:T(8,128)(2,1)S(1)}, u32[]{:S(2)}, u32[]{:S(2)}) collective-permute-start(bf16[1536,384]{1,0:T(8,128)(2,1)} %value.2), channel_id=1, source_target_pairs={{0,8},{8,0},{1,9},{9,1},{2,10},{10,2},{3,11},{11,3},{4,12},{12,4},... | collective-permute-start | bytes 3538952 | tf_op jit(solution)/shard_map/ppermute | solution.py:146
  17.8 9.1 %collective-permute-start.1 = (bf16[384,1536]{1,0:T(8,128)(2,1)}, bf16[384,1536]{1,0:T(8,128)(2,1)S(1)}, u32[]{:S(2)}, u32[]{:S(2)}) collective-permute-start(bf16[384,1536]{1,0:T(8,128)(2,1)} %value.3), channel_id=1, source_target_pairs={{0,8},{8,0},{1,9},{9,1},{2,10},{10,2},{3,11},{11,3},{4,12},{12,4},... | collective-permute-start | bytes 3538952 | tf_op jit(solution)/shard_map/ppermute | solution.py:146
  20.3 5.7 %collective-permute-start.2 = (f32[384]{0:T(512)S(1)}, f32[384]{0:T(512)S(1)}, u32[]{:S(2)}, u32[]{:S(2)}) collective-permute-start(f32[384]{0:T(512)S(1)} %copy-done.7), channel_id=1, source_target_pairs={{0,8},{8,0},{1,9},{9,1},{2,10},{10,2},{3,11},{11,3},{4,12},{12,4},... | collective-permute-start | bytes 4616 | tf_op jit(solution)/shard_map/ppermute | solution.py:146
  24.9 1.0 copy-start
  26.0 1.0 copy-start.2
  27.0 1.0 copy-start.5
  56.1 1.3 copy-start.3
  57.4 1.3 copy-start.1
  58.7 1.3 copy-start.6
  75.8 13.2 %collective-permute-start.3 = (bf16[64,1536]{1,0:T(8,128)(2,1)S(1)}, bf16[64,1536]{1,0:T(8,128)(2,1)S(1)}, u32[]{:S(2)}, u32[]{:S(2)}) collective-permute-start(bf16[64,1536]{1,0:T(8,128)(2,1)S(1)} %shard_map.90.mine), channel_id=1, source_target_pairs={{0,4},{4,0},{1,5},{5,1},{2,6},{6,2},{3,7},{7,3},{8,12},{12,8},{9,1... | collective-permute-start | bytes 589832 | tf_op jit(solution)/shard_map/ppermute | solution.py:161
  84.1 33.7 %collective-permute-start.4 = (bf16[256,3072]{1,0:T(8,128)(2,1)S(1)}, bf16[256,3072]{1,0:T(8,128)(2,1)}, u32[]{:S(2)}, u32[]{:S(2)}) collective-permute-start(bf16[256,3072]{1,0:T(8,128)(2,1)S(1)} %bitcast.8), channel_id=1, source_target_pairs={{0,8},{8,0},{1,9},{9,1},{2,10},{10,2},{3,11},{11,3},{4,12},{12,4},... | collective-permute-start | bytes 4718600 | tf_op jit(solution)/shard_map/ppermute | solution.py:146
  102.8 0.9 copy-start.4
  103.7 30.9 %all-to-all-start.3 = ((bf16[32,8,1536]{2,1,0:T(8,128)(2,1)}), bf16[32,8,1536]{2,1,0:T(8,128)(2,1)S(1)}, u32[]{:S(2)}, u32[]{:S(2)}) async-start(bf16[32,8,1536]{2,1,0:T(8,128)(2,1)} %bitcast.12), calls=%async_computation.3 | async-start | bytes 1572864 | tf_op jit(solution)/shard_map/all_to_all | solution.py:135
  113.4 5.8 %collective-permute-start.5 = (bf16[256,384]{1,0:T(8,128)(2,1)S(1)}, bf16[256,384]{1,0:T(8,128)(2,1)S(1)}, u32[]{:S(2)}, u32[]{:S(2)}) collective-permute-start(bf16[256,384]{1,0:T(8,128)(2,1)S(1)} %get-tuple-element.22), channel_id=1, source_target_pairs={{0,8},{8,0},{1,9},{9,1},{2,10},{10,2},{3,11},{11,3},{4,12},{12,4},... | collective-permute-start | bytes 589832 | tf_op jit(solution)/shard_map/ppermute | solution.py:146
  115.3 4.6 %collective-permute-start.6 = (bf16[256,384]{1,0:T(8,128)(2,1)S(1)}, bf16[256,384]{1,0:T(8,128)(2,1)S(1)}, u32[]{:S(2)}, u32[]{:S(2)}) collective-permute-start(bf16[256,384]{1,0:T(8,128)(2,1)S(1)} %get-tuple-element.21), channel_id=1, source_target_pairs={{0,8},{8,0},{1,9},{9,1},{2,10},{10,2},{3,11},{11,3},{4,12},{12,4},... | collective-permute-start | bytes 589832 | tf_op jit(solution)/shard_map/ppermute | solution.py:146

commit v5 on v4

--- a/solution.py
+++ b/solution.py
@@ -7,7 +7,12 @@
 
 BF16 = jnp.bfloat16
 F32 = jnp.float32
-PLANE = ("y", "zl")
+PLANE = "t"
+ORDER = (
+    19, 6, 9, 20, 24, 22, 27, 1, 10, 28, 3, 13, 2, 5, 18, 25, 23, 17, 7, 14, 31, 15,
+    26, 0, 12, 4, 11, 29, 16, 21, 8, 30,
+)
+GROUPS = [[2 * place + core for place in ORDER] for core in range(2)]
 MODEL = ("zh", "x")
 
 
@@ -132,18 +137,19 @@
 
 
 def exchange(blocks, axes):
-    return lax.all_to_all(blocks, axes, 0, 0, tiled=True)
+    groups = GROUPS if axes == PLANE else None
+    return lax.all_to_all(blocks, axes, 0, 0, axis_index_groups=groups, tiled=True)
 
 
 def sum_exchanged(value, axes):
-    count = lax.axis_size(axes)
+    count = len(ORDER) if axes == PLANE else lax.axis_size(axes)
     rows, columns = value.shape[0] // count, value.shape[1]
     blocks = exchange(value.reshape(count, rows, columns), axes)
     return call(sum_kernel, (rows, columns), (blocks,), [IN_VMEM])
 
 
 def swap_cores(value):
-    return jax.tree.map(lambda v: lax.ppermute(v, "co", [(0, 1), (1, 0)]), value)
+    return jax.tree.map(lambda v: lax.ppermute(v, PLANE, [(i, i ^ 1) for i in range(64)]), value)
 
 
 def body(acts, grad_out, w_in, b_in, w_out):
@@ -151,7 +157,7 @@
     others = swap_cores((w_in, w_out, b_in))
     staged = stage(w_in), stage(w_out)
     pair = jnp.concatenate([acts, grad_out], axis=1)
-    copies = jnp.broadcast_to(pair[None], (lax.axis_size(PLANE), *pair.shape))
+    copies = jnp.broadcast_to(pair[None], (len(ORDER), *pair.shape))
     tokens = exchange(copies, PLANE).reshape(-1, 2 * width)
     tokens, (w_in_other, w_out_other, b_in_other), (w_in, w_out) = (
         lax.optimization_barrier((tokens, others, staged))
@@ -185,8 +191,8 @@
 
 
 def solution(mesh):
-    fine = Mesh(mesh.devices.reshape(8, 4, 2, 2, 4), ("y", "zl", "co", "zh", "x"))
-    tokens = ("y", "zl", "co")
+    fine = Mesh(mesh.devices.reshape(64, 2, 4), ("t", "zh", "x"))
+    tokens = "t"
     return jax.shard_map(
         body,
         mesh=fine,

time: 136 us -> 132 us (0.971)
  the two profiles are of different devices: /device:TPU:16 before, /device:TPU:1 now
where the time goes in v5:
time: 132 us; the launch traced here: 131 us
  starting transfers between devices  56.5 us (43%)
  blocking collectives  26.6 us (20%)
  waiting for transfers between devices  25.5 us (19%)
  local copies, waits for them, and re-layouts  9.02 us (7%)
  Pallas kernels  7.06 us (5%)
  matrix products  3.86 us (3%)
  other arithmetic  1.44 us (1%)
    all_to_all x2, starting transfers between devices, exchange(): lax.all_to_all(blocks, axes, 0, 0, axis_index_groups=groups, tiled=True)  29.7 us
    all_to_all x2, blocking collectives, exchange(): lax.all_to_all(blocks, axes, 0, 0, axis_index_groups=groups, tiled=True)  26.6 us
    all_to_all x2, waiting for transfers between devices, exchange(): lax.all_to_all(blocks, axes, 0, 0, axis_index_groups=groups, tiled=True)  25.5 us
    ppermute x6, starting transfers between devices, swap_cores(): lax.ppermute(v, PLANE, [(i, i ^ 1) for i in range(64)])  18.8 us
    ppermute x1, starting transfers between devices, body(): other = lax.ppermute(mine, 'zh', [(0, 1), (1, 0)])  7.94 us
    pallas_call x10, Pallas kernels, call(): pl.pallas_call(kernel, out_shape=jax.ShapeDtypeStruct(shape, BF16), in_sp...  7.06 us
    unnamed x16, local copies, waits for them, and re-layouts  6 us
    dot_general x2, matrix products, contract_rows(): lax.dot_general(left, right, (((0,), (0,)), ((), ())), preferred_element_...  3.86 us
  transfers between devices with their start and end apart: 9, of which 2 were waited for; matrix products, arithmetic and copies ran while one was open for 5% of the time, Pallas kernels for 3%

profile of v5, /device:TPU:1, one launch (start us, length us, event | category | flops | bytes accessed | tf_op | source)
XLA Modules:
  0.0 130.9 jit_solution(12572672896429615858)
XLA Ops:
  0.6 0.8 pad_maximum_fusion.2
  1.4 1.4 %broadcast_in_dim.4 = bf16[32,8,3072]{2,1,0:T(8,128)(2,1)} broadcast(bf16[8,3072]{1,0:T(8,128)(2,1)S(1)} %pad_maximum_fusion.2), dimensions={1,2} | broadcast | bytes 1622016 | tf_op jit(solution)/shard_map/broadcast_in_dim | solution.py:160
  2.8 15.7 %all-to-all-start = ((bf16[32,8,3072]{2,1,0:T(8,128)(2,1)}), bf16[32,8,3072]{2,1,0:T(8,128)(2,1)S(1)}, u32[]{:S(2)}, u32[]{:S(2)}) async-start(bf16[32,8,3072]{2,1,0:T(8,128)(2,1)} %broadcast_in_dim.4), calls=%async_computation | async-start | bytes 3145728 | tf_op jit(solution)/shard_map/all_to_all | solution.py:141
  18.5 3.3 %collective-permute-start = (bf16[1536,384]{1,0:T(8,128)(2,1)}, bf16[1536,384]{1,0:T(8,128)(2,1)S(1)}, u32[]{:S(2)}, u32[]{:S(2)}) collective-permute-start(bf16[1536,384]{1,0:T(8,128)(2,1)} %value.2), channel_id=1, source_target_pairs={{0,8},{8,0},{16,24},{24,16},{32,40},{40,32},{48,56},{56,48},{64,72... | collective-permute-start | bytes 3538952 | tf_op jit(solution)/shard_map/ppermute | solution.py:152
  21.8 1.9 %collective-permute-start.1 = (bf16[384,1536]{1,0:T(8,128)(2,1)}, bf16[384,1536]{1,0:T(8,128)(2,1)S(1)}, u32[]{:S(2)}, u32[]{:S(2)}) collective-permute-start(bf16[384,1536]{1,0:T(8,128)(2,1)} %value.3), channel_id=1, source_target_pairs={{0,8},{8,0},{16,24},{24,16},{32,40},{40,32},{48,56},{56,48},{64,72... | collective-permute-start | bytes 3538952 | tf_op jit(solution)/shard_map/ppermute | solution.py:152
  23.7 2.4 %collective-permute-start.2 = (f32[384]{0:T(512)S(1)}, f32[384]{0:T(512)S(1)}, u32[]{:S(2)}, u32[]{:S(2)}) collective-permute-start(f32[384]{0:T(512)S(1)} %copy-done.7), channel_id=1, source_target_pairs={{0,8},{8,0},{16,24},{24,16},{32,40},{40,32},{48,56},{56,48},{64,72... | collective-permute-start | bytes 4616 | tf_op jit(solution)/shard_map/ppermute | solution.py:152
  26.1 1.4 %shard_map.84.weight.own = bf16[1536,384]{1,0:T(8,128)(2,1)S(1)} custom-call(bf16[1536,384]{1,0:T(8,128)(2,1)} %value.2), custom_call_target="tpu_custom_call" | custom-call | bytes 1179648 | tf_op jit(solution)/shard_map/pallas_call | solution.py:46
  27.5 1.3 %shard_map.85.weight = bf16[384,1536]{1,0:T(8,128)(2,1)S(1)} custom-call(bf16[384,1536]{1,0:T(8,128)(2,1)} %value.3), custom_call_target="tpu_custom_call" | custom-call | bytes 1179648 | tf_op jit(solution)/shard_map/pallas_call | solution.py:46
  28.9 1.0 copy-done
  29.9 1.0 copy-done.2
  30.9 1.0 copy-done.5
  31.9 21.7 %all-to-all-done = bf16[32,8,3072]{2,1,0:T(8,128)(2,1)S(1)} async-done(((bf16[32,8,3072]{2,1,0:T(8,128)(2,1)}), bf16[32,8,3072]{2,1,0:T(8,128)(2,1)S(1)}, u32[]{:S(2)}, u32[]{:S(2)}) %all-to-all-start) | async-done | bytes 1572896 | tf_op jit(solution)/shard_map/all_to_all | solution.py:141
  54.2 0.7 copy-done.3
  55.4 0.7 copy-done.1
  56.1 0.6 shard_map.88.refs_2_
  56.7 0.7 copy-done.6
  57.4 0.6 shard_map.89
  58.1 15.1 %all_to_all.20.blocks = bf16[4,64,1536]{2,1,0:T(8,128)(2,1)S(1)} all-to-all(bf16[4,64,1536]{2,1,0:T(8,128)(2,1)S(1)} %bitcast.13), channel_id=1, replica_groups=mesh['gx'=8,'gy'=8,'gz'=8] {'gz':(2)4}, dimensions={0} | all-to-all | bytes 1572864 | tf_op jit(solution)/shard_map/all_to_all | solution.py:141
  73.2 7.9 %collective-permute-start.3 = (bf16[64,1536]{1,0:T(8,128)(2,1)S(1)}, bf16[64,1536]{1,0:T(8,128)(2,1)S(1)}, u32[]{:S(2)}, u32[]{:S(2)}) collective-permute-start(bf16[64,1536]{1,0:T(8,128)(2,1)S(1)} %shard_map.90.mine), channel_id=1, source_target_pairs={{0,4},{4,0},{1,5},{5,1},{2,6},{6,2},{3,7},{7,3},{8,12},{12,8},{9,1... | collective-permute-start | bytes 589832 | tf_op jit(solution)/shard_map/ppermute | solution.py:167
  81.2 4.8 %collective-permute-start.4 = (bf16[256,3072]{1,0:T(8,128)(2,1)S(1)}, bf16[256,3072]{1,0:T(8,128)(2,1)}, u32[]{:S(2)}, u32[]{:S(2)}) collective-permute-start(bf16[256,3072]{1,0:T(8,128)(2,1)S(1)} %bitcast.8), channel_id=1, source_target_pairs={{0,8},{8,0},{16,24},{24,16},{32,40},{40,32},{48,56},{56,48},{64,72... | collective-permute-start | bytes 4718600 | tf_op jit(solution)/shard_map/ppermute | solution.py:152
  86.2 11.5 %all_to_all.21 = bf16[4,64,1536]{2,1,0:T(8,128)(2,1)S(1)} all-to-all(bf16[4,64,1536]{2,1,0:T(8,128)(2,1)S(1)} %shard_map.91), channel_id=1, replica_groups=mesh['gx'=8,'gy'=8,'gz'=8] {'gz':(2)4}, dimensions={0} | all-to-all | bytes 1572864 | tf_op jit(solution)/shard_map/all_to_all | solution.py:141
  97.7 1.0 shard_map.92
  98.7 0.9 copy-done.4
  99.6 14.0 %all-to-all-start.3 = ((bf16[32,8,1536]{2,1,0:T(8,128)(2,1)}), bf16[32,8,1536]{2,1,0:T(8,128)(2,1)S(1)}, u32[]{:S(2)}, u32[]{:S(2)}) async-start(bf16[32,8,1536]{2,1,0:T(8,128)(2,1)} %bitcast.12), calls=%async_computation.3 | async-start | bytes 1572864 | tf_op jit(solution)/shard_map/all_to_all | solution.py:141
  113.8 4.5 %collective-permute-start.5 = (bf16[256,384]{1,0:T(8,128)(2,1)S(1)}, bf16[256,384]{1,0:T(8,128)(2,1)S(1)}, u32[]{:S(2)}, u32[]{:S(2)}) collective-permute-start(bf16[256,384]{1,0:T(8,128)(2,1)S(1)} %get-tuple-element.22), channel_id=1, source_target_pairs={{0,8},{8,0},{16,24},{24,16},{32,40},{40,32},{48,56},{56,48},{64,72... | collective-permute-start | bytes 589832 | tf_op jit(solution)/shard_map/ppermute | solution.py:152
  118.3 1.9 %collective-permute-start.6 = (bf16[256,384]{1,0:T(8,128)(2,1)S(1)}, bf16[256,384]{1,0:T(8,128)(2,1)S(1)}, u32[]{:S(2)}, u32[]{:S(2)}) collective-permute-start(bf16[256,384]{1,0:T(8,128)(2,1)S(1)} %get-tuple-element.21), channel_id=1, source_target_pairs={{0,8},{8,0},{16,24},{24,16},{32,40},{40,32},{48,56},{56,48},{64,72... | collective-permute-start | bytes 589832 | tf_op jit(solution)/shard_map/ppermute | solution.py:152
  120.2 1.5 %fusion.12 = (bf16[256,1536]{1,0:T(8,128)(2,1)S(1)}, bf16[256,1536]{1,0:T(8,128)(2,1)S(1)}) fusion(bf16[256,3072]{1,0:T(8,128)(2,1)} %collective-permute-done.4), kind=kLoop, calls=%fused_computation.18 | loop fusion | bytes 3145728 | tf_op jit(solution)/shard_map/slice | solution.py:184
  121.7 0.7 convert_reduce_fusion
  122.4 1.8 %convolution_convert_fusion = bf16[384,1536]{1,0:T(8,128)(2,1)} fusion(bf16[256,1536]{1,0:T(8,128)(2,1)S(1)} %get-tuple-element.18, bf16[256,1536]{1,0:T(8,128)(2,1)S(1)} %get-tuple-element.16, bf16[256,384]{1,0:T(8,128)(2,1)S(1)} %collective-permute-done.6, bf16[256,384]{1,0:T(8,128)(2,1)S(1)} %get-tuple-element.20), kind=kOutput, calls=%fused_computation | convolution fusion | flops 608501760 | bytes 3145728 | tf_op jit(solution)/shard_map/dot_general | solution.py:28
  124.2 2.0 %convolution_convert_fusion.1 = bf16[1536,384]{1,0:T(8,128)(2,1)} fusion(bf16[256,1536]{1,0:T(8,128)(2,1)S(1)} %get-tuple-element.19, bf16[256,1536]{1,0:T(8,128)(2,1)S(1)} %get-tuple-element.17, bf16[256,384]{1,0:T(8,128)(2,1)S(1)} %collective-permute-done.5, bf16[256,384]{1,0:T(8,128)(2,1)S(1)} %get-tuple-element.23), kind=kOutput, calls=%fused_computation.1 | convolution fusion | flops 608501760 | bytes 3145728 | tf_op jit(solution)/shard_map/dot_general | solution.py:28
  126.3 3.9 %all-to-all-done.3.blocks = bf16[32,8,1536]{2,1,0:T(8,128)(2,1)S(1)} async-done(((bf16[32,8,1536]{2,1,0:T(8,128)(2,1)}), bf16[32,8,1536]{2,1,0:T(8,128)(2,1)S(1)}, u32[]{:S(2)}, u32[]{:S(2)}) %all-to-all-start.3) | async-done | bytes 786464 | tf_op jit(solution)/shard_map/all_to_all | solution.py:141
  130.1 0.7 shard_map.93
  (24 shorter events, 1.6 us)
Async XLA Ops:
  2.7 21.0 %copy-start.7 = (f32[384]{0:T(512)S(1)}, f32[384]{0:T(512)}, u32[]{:S(2)}) copy-start(f32[384]{0:T(512)} %param.8) | copy-start | bytes 4612
  2.8 50.8 %all-to-all-start = ((bf16[32,8,3072]{2,1,0:T(8,128)(2,1)}), bf16[32,8,3072]{2,1,0:T(8,128)(2,1)S(1)}, u32[]{:S(2)}, u32[]{:S(2)}) async-start(bf16[32,8,3072]{2,1,0:T(8,128)(2,1)} %broadcast_in_dim.4), calls=%async_computation | async-start | bytes 3145728 | tf_op jit(solution)/shard_map/all_to_all | solution.py:141
  18.5 11.4 %collective-permute-start = (bf16[1536,384]{1,0:T(8,128)(2,1)}, bf16[1536,384]{1,0:T(8,128)(2,1)S(1)}, u32[]{:S(2)}, u32[]{:S(2)}) collective-permute-start(bf16[1536,384]{1,0:T(8,128)(2,1)} %value.2), channel_id=1, source_target_pairs={{0,8},{8,0},{16,24},{24,16},{32,40},{40,32},{48,56},{56,48},{64,72... | collective-permute-start | bytes 3538952 | tf_op jit(solution)/shard_map/ppermute | solution.py:152
  21.8 9.1 %collective-permute-start.1 = (bf16[384,1536]{1,0:T(8,128)(2,1)}, bf16[384,1536]{1,0:T(8,128)(2,1)S(1)}, u32[]{:S(2)}, u32[]{:S(2)}) collective-permute-start(bf16[384,1536]{1,0:T(8,128)(2,1)} %value.3), channel_id=1, source_target_pairs={{0,8},{8,0},{16,24},{24,16},{32,40},{40,32},{48,56},{56,48},{64,72... | collective-permute-start | bytes 3538952 | tf_op jit(solution)/shard_map/ppermute | solution.py:152
  23.7 6.2 %collective-permute-start.2 = (f32[384]{0:T(512)S(1)}, f32[384]{0:T(512)S(1)}, u32[]{:S(2)}, u32[]{:S(2)}) collective-permute-start(f32[384]{0:T(512)S(1)} %copy-done.7), channel_id=1, source_target_pairs={{0,8},{8,0},{16,24},{24,16},{32,40},{40,32},{48,56},{56,48},{64,72... | collective-permute-start | bytes 4616 | tf_op jit(solution)/shard_map/ppermute | solution.py:152
  28.9 1.0 copy-start
  29.9 1.0 copy-start.2
  30.9 1.0 copy-start.5
  53.6 1.3 copy-start.3
  54.9 1.3 copy-start.1
  56.1 1.3 copy-start.6
  73.2 12.8 %collective-permute-start.3 = (bf16[64,1536]{1,0:T(8,128)(2,1)S(1)}, bf16[64,1536]{1,0:T(8,128)(2,1)S(1)}, u32[]{:S(2)}, u32[]{:S(2)}) collective-permute-start(bf16[64,1536]{1,0:T(8,128)(2,1)S(1)} %shard_map.90.mine), channel_id=1, source_target_pairs={{0,4},{4,0},{1,5},{5,1},{2,6},{6,2},{3,7},{7,3},{8,12},{12,8},{9,1... | collective-permute-start | bytes 589832 | tf_op jit(solution)/shard_map/ppermute | solution.py:167
  81.2 39.1 %collective-permute-start.4 = (bf16[256,3072]{1,0:T(8,128)(2,1)S(1)}, bf16[256,3072]{1,0:T(8,128)(2,1)}, u32[]{:S(2)}, u32[]{:S(2)}) collective-permute-start(bf16[256,3072]{1,0:T(8,128)(2,1)S(1)} %bitcast.8), channel_id=1, source_target_pairs={{0,8},{8,0},{16,24},{24,16},{32,40},{40,32},{48,56},{56,48},{64,72... | collective-permute-start | bytes 4718600 | tf_op jit(solution)/shard_map/ppermute | solution.py:152
  98.7 0.9 copy-start.4
  99.6 30.5 %all-to-all-start.3 = ((bf16[32,8,1536]{2,1,0:T(8,128)(2,1)}), bf16[32,8,1536]{2,1,0:T(8,128)(2,1)S(1)}, u32[]{:S(2)}, u32[]{:S(2)}) async-start(bf16[32,8,1536]{2,1,0:T(8,128)(2,1)} %bitcast.12), calls=%async_computation.3 | async-start | bytes 1572864 | tf_op jit(solution)/shard_map/all_to_all | solution.py:141
  113.8 7.9 %collective-permute-start.5 = (bf16[256,384]{1,0:T(8,128)(2,1)S(1)}, bf16[256,384]{1,0:T(8,128)(2,1)S(1)}, u32[]{:S(2)}, u32[]{:S(2)}) collective-permute-start(bf16[256,384]{1,0:T(8,128)(2,1)S(1)} %get-tuple-element.22), channel_id=1, source_target_pairs={{0,8},{8,0},{16,24},{24,16},{32,40},{40,32},{48,56},{56,48},{64,72... | collective-permute-start | bytes 589832 | tf_op jit(solution)/shard_map/ppermute | solution.py:152
  118.3 4.1 %collective-permute-start.6 = (bf16[256,384]{1,0:T(8,128)(2,1)S(1)}, bf16[256,384]{1,0:T(8,128)(2,1)S(1)}, u32[]{:S(2)}, u32[]{:S(2)}) collective-permute-start(bf16[256,384]{1,0:T(8,128)(2,1)S(1)} %get-tuple-element.21), channel_id=1, source_target_pairs={{0,8},{8,0},{16,24},{24,16},{32,40},{40,32},{48,56},{56,48},{64,72... | collective-permute-start | bytes 589832 | tf_op jit(solution)/shard_map/ppermute | solution.py:152

commit v6 on v5

--- a/solution.py
+++ b/solution.py
@@ -9,8 +9,8 @@
 F32 = jnp.float32
 PLANE = "t"
 ORDER = (
-    19, 6, 9, 20, 24, 22, 27, 1, 10, 28, 3, 13, 2, 5, 18, 25, 23, 17, 7, 14, 31, 15,
-    26, 0, 12, 4, 11, 29, 16, 21, 8, 30,
+    31, 23, 18, 4, 12, 21, 8, 19, 28, 3, 2, 1, 24, 26, 14, 11, 17, 0, 7, 27, 29, 5,
+    16, 25, 6, 15, 9, 20, 30, 22, 13, 10,
 )
 GROUPS = [[2 * place + core for place in ORDER] for core in range(2)]
 MODEL = ("zh", "x")

time: 132 us -> 132 us (level)
  waiting for transfers between devices: 25.5 us -> 30.7 us
  starting transfers between devices: 56.5 us -> 52.4 us
    all_to_all x2, starting transfers between devices: 29.7 us -> 24.5 us  [exchange(): lax.all_to_all(blocks, axes, 0, 0, axis_index_groups=groups, tiled=True)]
    all_to_all x2, waiting for transfers between devices: 25.5 us -> 30.3 us  [exchange(): lax.all_to_all(blocks, axes, 0, 0, axis_index_groups=groups, tiled=True)]
  transfers between devices with their start and end apart: 9 -> 9, of which waited for: 2 -> 3; matrix products, arithmetic and copies ran while one was open for 5% -> 5% of each run, Pallas kernels for 3% -> 3%
where the time goes in v6:
time: 132 us; the launch traced here: 131 us
  starting transfers between devices  52.4 us (40%)
  waiting for transfers between devices  30.7 us (23%)
  blocking collectives  26.1 us (20%)
  local copies, waits for them, and re-layouts  9.01 us (7%)
  Pallas kernels  7.06 us (5%)
  matrix products  3.86 us (3%)
  other arithmetic  1.44 us (1%)
    all_to_all x2, waiting for transfers between devices, exchange(): lax.all_to_all(blocks, axes, 0, 0, axis_index_groups=groups, tiled=True)  30.3 us
    all_to_all x2, blocking collectives, exchange(): lax.all_to_all(blocks, axes, 0, 0, axis_index_groups=groups, tiled=True)  26.1 us
    all_to_all x2, starting transfers between devices, exchange(): lax.all_to_all(blocks, axes, 0, 0, axis_index_groups=groups, tiled=True)  24.5 us
    ppermute x6, starting transfers between devices, swap_cores(): lax.ppermute(v, PLANE, [(i, i ^ 1) for i in range(64)])  19.9 us
    ppermute x1, starting transfers between devices, body(): other = lax.ppermute(mine, 'zh', [(0, 1), (1, 0)])  7.95 us
    pallas_call x10, Pallas kernels, call(): pl.pallas_call(kernel, out_shape=jax.ShapeDtypeStruct(shape, BF16), in_sp...  7.06 us
    unnamed x16, local copies, waits for them, and re-layouts  5.99 us
    dot_general x2, matrix products, contract_rows(): lax.dot_general(left, right, (((0,), (0,)), ((), ())), preferred_element_...  3.86 us
  transfers between devices with their start and end apart: 9, of which 3 were waited for; matrix products, arithmetic and copies ran while one was open for 5% of the time, Pallas kernels for 3%

profile of v6, /device:TPU:1, one launch (start us, length us, event | category | flops | bytes accessed | tf_op | source)
XLA Modules:
  0.0 131.4 jit_solution(16587942164256764568)
XLA Ops:
  0.6 0.8 pad_maximum_fusion.2
  1.4 1.4 %broadcast_in_dim.4 = bf16[32,8,3072]{2,1,0:T(8,128)(2,1)} broadcast(bf16[8,3072]{1,0:T(8,128)(2,1)S(1)} %pad_maximum_fusion.2), dimensions={1,2} | broadcast | bytes 1622016 | tf_op jit(solution)/shard_map/broadcast_in_dim | solution.py:160
  2.8 13.7 %all-to-all-start = ((bf16[32,8,3072]{2,1,0:T(8,128)(2,1)}), bf16[32,8,3072]{2,1,0:T(8,128)(2,1)S(1)}, u32[]{:S(2)}, u32[]{:S(2)}) async-start(bf16[32,8,3072]{2,1,0:T(8,128)(2,1)} %broadcast_in_dim.4), calls=%async_computation | async-start | bytes 3145728 | tf_op jit(solution)/shard_map/all_to_all | solution.py:141
  16.4 3.1 %collective-permute-start = (bf16[1536,384]{1,0:T(8,128)(2,1)}, bf16[1536,384]{1,0:T(8,128)(2,1)S(1)}, u32[]{:S(2)}, u32[]{:S(2)}) collective-permute-start(bf16[1536,384]{1,0:T(8,128)(2,1)} %value.2), channel_id=1, source_target_pairs={{0,8},{8,0},{16,24},{24,16},{32,40},{40,32},{48,56},{56,48},{64,72... | collective-permute-start | bytes 3538952 | tf_op jit(solution)/shard_map/ppermute | solution.py:152
  19.6 1.9 %collective-permute-start.1 = (bf16[384,1536]{1,0:T(8,128)(2,1)}, bf16[384,1536]{1,0:T(8,128)(2,1)S(1)}, u32[]{:S(2)}, u32[]{:S(2)}) collective-permute-start(bf16[384,1536]{1,0:T(8,128)(2,1)} %value.3), channel_id=1, source_target_pairs={{0,8},{8,0},{16,24},{24,16},{32,40},{40,32},{48,56},{56,48},{64,72... | collective-permute-start | bytes 3538952 | tf_op jit(solution)/shard_map/ppermute | solution.py:152
  21.5 2.4 %collective-permute-start.2 = (f32[384]{0:T(512)S(1)}, f32[384]{0:T(512)S(1)}, u32[]{:S(2)}, u32[]{:S(2)}) collective-permute-start(f32[384]{0:T(512)S(1)} %copy-done.7), channel_id=1, source_target_pairs={{0,8},{8,0},{16,24},{24,16},{32,40},{40,32},{48,56},{56,48},{64,72... | collective-permute-start | bytes 4616 | tf_op jit(solution)/shard_map/ppermute | solution.py:152
  23.9 1.4 %shard_map.84.weight.own = bf16[1536,384]{1,0:T(8,128)(2,1)S(1)} custom-call(bf16[1536,384]{1,0:T(8,128)(2,1)} %value.2), custom_call_target="tpu_custom_call" | custom-call | bytes 1179648 | tf_op jit(solution)/shard_map/pallas_call | solution.py:46
  25.3 1.3 %shard_map.85.weight = bf16[384,1536]{1,0:T(8,128)(2,1)S(1)} custom-call(bf16[384,1536]{1,0:T(8,128)(2,1)} %value.3), custom_call_target="tpu_custom_call" | custom-call | bytes 1179648 | tf_op jit(solution)/shard_map/pallas_call | solution.py:46
  26.7 1.0 copy-done
  27.7 1.0 copy-done.2
  28.7 1.0 copy-done.5
  29.7 24.5 %all-to-all-done = bf16[32,8,3072]{2,1,0:T(8,128)(2,1)S(1)} async-done(((bf16[32,8,3072]{2,1,0:T(8,128)(2,1)}), bf16[32,8,3072]{2,1,0:T(8,128)(2,1)S(1)}, u32[]{:S(2)}, u32[]{:S(2)}) %all-to-all-start) | async-done | bytes 1572896 | tf_op jit(solution)/shard_map/all_to_all | solution.py:141
  54.8 0.7 copy-done.3
  56.1 0.7 copy-done.1
  56.8 0.6 shard_map.88.refs_2_
  57.4 0.7 copy-done.6
  58.0 0.7 shard_map.89
  58.7 13.7 %all_to_all.20.blocks = bf16[4,64,1536]{2,1,0:T(8,128)(2,1)S(1)} all-to-all(bf16[4,64,1536]{2,1,0:T(8,128)(2,1)S(1)} %bitcast.13), channel_id=1, replica_groups=mesh['gx'=8,'gy'=8,'gz'=8] {'gz':(2)4}, dimensions={0} | all-to-all | bytes 1572864 | tf_op jit(solution)/shard_map/all_to_all | solution.py:141
  72.5 8.0 %collective-permute-start.3 = (bf16[64,1536]{1,0:T(8,128)(2,1)S(1)}, bf16[64,1536]{1,0:T(8,128)(2,1)S(1)}, u32[]{:S(2)}, u32[]{:S(2)}) collective-permute-start(bf16[64,1536]{1,0:T(8,128)(2,1)S(1)} %shard_map.90.mine), channel_id=1, source_target_pairs={{0,4},{4,0},{1,5},{5,1},{2,6},{6,2},{3,7},{7,3},{8,12},{12,8},{9,1... | collective-permute-start | bytes 589832 | tf_op jit(solution)/shard_map/ppermute | solution.py:167
  80.5 5.5 %collective-permute-start.4 = (bf16[256,3072]{1,0:T(8,128)(2,1)S(1)}, bf16[256,3072]{1,0:T(8,128)(2,1)}, u32[]{:S(2)}, u32[]{:S(2)}) collective-permute-start(bf16[256,3072]{1,0:T(8,128)(2,1)S(1)} %bitcast.8), channel_id=1, source_target_pairs={{0,8},{8,0},{16,24},{24,16},{32,40},{40,32},{48,56},{56,48},{64,72... | collective-permute-start | bytes 4718600 | tf_op jit(solution)/shard_map/ppermute | solution.py:152
  86.5 12.3 %all_to_all.21 = bf16[4,64,1536]{2,1,0:T(8,128)(2,1)S(1)} all-to-all(bf16[4,64,1536]{2,1,0:T(8,128)(2,1)S(1)} %shard_map.91), channel_id=1, replica_groups=mesh['gx'=8,'gy'=8,'gz'=8] {'gz':(2)4}, dimensions={0} | all-to-all | bytes 1572864 | tf_op jit(solution)/shard_map/all_to_all | solution.py:141
  98.9 1.0 shard_map.92
  99.9 0.9 copy-done.4
  100.8 10.9 %all-to-all-start.3 = ((bf16[32,8,1536]{2,1,0:T(8,128)(2,1)}), bf16[32,8,1536]{2,1,0:T(8,128)(2,1)S(1)}, u32[]{:S(2)}, u32[]{:S(2)}) async-start(bf16[32,8,1536]{2,1,0:T(8,128)(2,1)} %bitcast.12), calls=%async_computation.3 | async-start | bytes 1572864 | tf_op jit(solution)/shard_map/all_to_all | solution.py:141
  111.9 5.0 %collective-permute-start.5 = (bf16[256,384]{1,0:T(8,128)(2,1)S(1)}, bf16[256,384]{1,0:T(8,128)(2,1)S(1)}, u32[]{:S(2)}, u32[]{:S(2)}) collective-permute-start(bf16[256,384]{1,0:T(8,128)(2,1)S(1)} %get-tuple-element.22), channel_id=1, source_target_pairs={{0,8},{8,0},{16,24},{24,16},{32,40},{40,32},{48,56},{56,48},{64,72... | collective-permute-start | bytes 589832 | tf_op jit(solution)/shard_map/ppermute | solution.py:152
  116.9 1.9 %collective-permute-start.6 = (bf16[256,384]{1,0:T(8,128)(2,1)S(1)}, bf16[256,384]{1,0:T(8,128)(2,1)S(1)}, u32[]{:S(2)}, u32[]{:S(2)}) collective-permute-start(bf16[256,384]{1,0:T(8,128)(2,1)S(1)} %get-tuple-element.21), channel_id=1, source_target_pairs={{0,8},{8,0},{16,24},{24,16},{32,40},{40,32},{48,56},{56,48},{64,72... | collective-permute-start | bytes 589832 | tf_op jit(solution)/shard_map/ppermute | solution.py:152
  118.8 1.5 %fusion.12 = (bf16[256,1536]{1,0:T(8,128)(2,1)S(1)}, bf16[256,1536]{1,0:T(8,128)(2,1)S(1)}) fusion(bf16[256,3072]{1,0:T(8,128)(2,1)} %collective-permute-done.4), kind=kLoop, calls=%fused_computation.18 | loop fusion | bytes 3145728 | tf_op jit(solution)/shard_map/slice | solution.py:184
  120.3 0.7 convert_reduce_fusion
  121.0 1.8 %convolution_convert_fusion = bf16[384,1536]{1,0:T(8,128)(2,1)} fusion(bf16[256,1536]{1,0:T(8,128)(2,1)S(1)} %get-tuple-element.18, bf16[256,1536]{1,0:T(8,128)(2,1)S(1)} %get-tuple-element.16, bf16[256,384]{1,0:T(8,128)(2,1)S(1)} %collective-permute-done.6, bf16[256,384]{1,0:T(8,128)(2,1)S(1)} %get-tuple-element.20), kind=kOutput, calls=%fused_computation | convolution fusion | flops 608501760 | bytes 3145728 | tf_op jit(solution)/shard_map/dot_general | solution.py:28
  122.8 2.0 %convolution_convert_fusion.1 = bf16[1536,384]{1,0:T(8,128)(2,1)} fusion(bf16[256,1536]{1,0:T(8,128)(2,1)S(1)} %get-tuple-element.19, bf16[256,1536]{1,0:T(8,128)(2,1)S(1)} %get-tuple-element.17, bf16[256,384]{1,0:T(8,128)(2,1)S(1)} %collective-permute-done.5, bf16[256,384]{1,0:T(8,128)(2,1)S(1)} %get-tuple-element.23), kind=kOutput, calls=%fused_computation.1 | convolution fusion | flops 608501760 | bytes 3145728 | tf_op jit(solution)/shard_map/dot_general | solution.py:28
  124.8 5.8 %all-to-all-done.3.blocks = bf16[32,8,1536]{2,1,0:T(8,128)(2,1)S(1)} async-done(((bf16[32,8,1536]{2,1,0:T(8,128)(2,1)}), bf16[32,8,1536]{2,1,0:T(8,128)(2,1)S(1)}, u32[]{:S(2)}, u32[]{:S(2)}) %all-to-all-start.3) | async-done | bytes 786464 | tf_op jit(solution)/shard_map/all_to_all | solution.py:141
  130.6 0.7 shard_map.93
  (24 shorter events, 2.0 us)
Async XLA Ops:
  2.7 18.8 %copy-start.7 = (f32[384]{0:T(512)S(1)}, f32[384]{0:T(512)}, u32[]{:S(2)}) copy-start(f32[384]{0:T(512)} %param.8) | copy-start | bytes 4612
  2.8 51.5 %all-to-all-start = ((bf16[32,8,3072]{2,1,0:T(8,128)(2,1)}), bf16[32,8,3072]{2,1,0:T(8,128)(2,1)S(1)}, u32[]{:S(2)}, u32[]{:S(2)}) async-start(bf16[32,8,3072]{2,1,0:T(8,128)(2,1)} %broadcast_in_dim.4), calls=%async_computation | async-start | bytes 3145728 | tf_op jit(solution)/shard_map/all_to_all | solution.py:141
  16.4 11.3 %collective-permute-start = (bf16[1536,384]{1,0:T(8,128)(2,1)}, bf16[1536,384]{1,0:T(8,128)(2,1)S(1)}, u32[]{:S(2)}, u32[]{:S(2)}) collective-permute-start(bf16[1536,384]{1,0:T(8,128)(2,1)} %value.2), channel_id=1, source_target_pairs={{0,8},{8,0},{16,24},{24,16},{32,40},{40,32},{48,56},{56,48},{64,72... | collective-permute-start | bytes 3538952 | tf_op jit(solution)/shard_map/ppermute | solution.py:152
  19.6 9.1 %collective-permute-start.1 = (bf16[384,1536]{1,0:T(8,128)(2,1)}, bf16[384,1536]{1,0:T(8,128)(2,1)S(1)}, u32[]{:S(2)}, u32[]{:S(2)}) collective-permute-start(bf16[384,1536]{1,0:T(8,128)(2,1)} %value.3), channel_id=1, source_target_pairs={{0,8},{8,0},{16,24},{24,16},{32,40},{40,32},{48,56},{56,48},{64,72... | collective-permute-start | bytes 3538952 | tf_op jit(solution)/shard_map/ppermute | solution.py:152
  21.5 6.2 %collective-permute-start.2 = (f32[384]{0:T(512)S(1)}, f32[384]{0:T(512)S(1)}, u32[]{:S(2)}, u32[]{:S(2)}) collective-permute-start(f32[384]{0:T(512)S(1)} %copy-done.7), channel_id=1, source_target_pairs={{0,8},{8,0},{16,24},{24,16},{32,40},{40,32},{48,56},{56,48},{64,72... | collective-permute-start | bytes 4616 | tf_op jit(solution)/shard_map/ppermute | solution.py:152
  26.7 1.0 copy-start
  27.7 1.0 copy-start.2
  28.7 1.0 copy-start.5
  54.2 1.3 copy-start.3
  55.5 1.3 copy-start.1
  56.8 1.3 copy-start.6
  72.5 13.9 %collective-permute-start.3 = (bf16[64,1536]{1,0:T(8,128)(2,1)S(1)}, bf16[64,1536]{1,0:T(8,128)(2,1)S(1)}, u32[]{:S(2)}, u32[]{:S(2)}) collective-permute-start(bf16[64,1536]{1,0:T(8,128)(2,1)S(1)} %shard_map.90.mine), channel_id=1, source_target_pairs={{0,4},{4,0},{1,5},{5,1},{2,6},{6,2},{3,7},{7,3},{8,12},{12,8},{9,1... | collective-permute-start | bytes 589832 | tf_op jit(solution)/shard_map/ppermute | solution.py:167
  80.5 38.3 %collective-permute-start.4 = (bf16[256,3072]{1,0:T(8,128)(2,1)S(1)}, bf16[256,3072]{1,0:T(8,128)(2,1)}, u32[]{:S(2)}, u32[]{:S(2)}) collective-permute-start(bf16[256,3072]{1,0:T(8,128)(2,1)S(1)} %bitcast.8), channel_id=1, source_target_pairs={{0,8},{8,0},{16,24},{24,16},{32,40},{40,32},{48,56},{56,48},{64,72... | collective-permute-start | bytes 4718600 | tf_op jit(solution)/shard_map/ppermute | solution.py:152
  99.9 0.9 copy-start.4
  100.8 29.9 %all-to-all-start.3 = ((bf16[32,8,1536]{2,1,0:T(8,128)(2,1)}), bf16[32,8,1536]{2,1,0:T(8,128)(2,1)S(1)}, u32[]{:S(2)}, u32[]{:S(2)}) async-start(bf16[32,8,1536]{2,1,0:T(8,128)(2,1)} %bitcast.12), calls=%async_computation.3 | async-start | bytes 1572864 | tf_op jit(solution)/shard_map/all_to_all | solution.py:141
  111.9 8.4 %collective-permute-start.5 = (bf16[256,384]{1,0:T(8,128)(2,1)S(1)}, bf16[256,384]{1,0:T(8,128)(2,1)S(1)}, u32[]{:S(2)}, u32[]{:S(2)}) collective-permute-start(bf16[256,384]{1,0:T(8,128)(2,1)S(1)} %get-tuple-element.22), channel_id=1, source_target_pairs={{0,8},{8,0},{16,24},{24,16},{32,40},{40,32},{48,56},{56,48},{64,72... | collective-permute-start | bytes 589832 | tf_op jit(solution)/shard_map/ppermute | solution.py:152
  116.9 4.1 %collective-permute-start.6 = (bf16[256,384]{1,0:T(8,128)(2,1)S(1)}, bf16[256,384]{1,0:T(8,128)(2,1)S(1)}, u32[]{:S(2)}, u32[]{:S(2)}) collective-permute-start(bf16[256,384]{1,0:T(8,128)(2,1)S(1)} %get-tuple-element.21), channel_id=1, source_target_pairs={{0,8},{8,0},{16,24},{24,16},{32,40},{40,32},{48,56},{56,48},{64,72... | collective-permute-start | bytes 589832 | tf_op jit(solution)/shard_map/ppermute | solution.py:152
